TPU v7x, 128 devices: a whole 4x4x4 slice. The times are simulated.
128 devices in a mesh: ctx: 16 (over y_hi, z, core), chan: 8 (over x, y_lo).
Axes of the slice: x: 4, y: 4 (y_hi: 2, y_lo: 2; y = y_hi * 2 + y_lo), z: 4, core: 2. Of those that a mesh axis runs over, the one named last changes fastest.
Arguments:
- tokens: bfloat16 [1, 262144, 768], P(None, ('ctx', 'chan')), may hold values from -6 to 6
- norm_gain: float32 [768], replicated, may hold values from 0.1 to 1.9
- block_weights: bfloat16 [512, 512, 512], P(('ctx', 'chan')), may hold values from -0.25 to 0.25
- stride_weights: bfloat16 [512, 512, 512], P(('ctx', 'chan')), may hold values from -0.25 to 0.25
- proj_weights: bfloat16 [3, 768, 768], P(None, 'chan'), may hold values from -11 to 11
- proj_scales: float32 [3, 768], replicated, may hold values from 0.5 to 2
Outputs:
- layer_output: bfloat16 [1, 262144, 768], P(None, ('ctx', 'chan'))
All inputs are finite; a program needn't handle non-finite values.
Results may differ from a plain program's by a relative error of at most 0.017.
Values may be sent and summed in bfloat16 or wider, within the bound.
A program may use at most 128 MiB of HBM per device.

v0:
```python
import jax
import jax.numpy as jnp
from jax import lax
from jax.sharding import PartitionSpec as P


def column_scale(raw_sums, scales):
    return scales * lax.rsqrt(raw_sums + 1e-06)


def first_factor(value, block_weights):
    n_seqs, n_rows, channels = value.shape
    local_blocks, block_size = (block_weights.shape[0], block_weights.shape[1])
    grouped = value.reshape(n_seqs, local_blocks, block_size, channels)
    return jnp.einsum(
        "bts,nbsc->nbtc", block_weights, grouped, preferred_element_type=jnp.float32
    ).astype(jnp.bfloat16)


def local(tokens, norm_gain, block_weights, stride_weights, proj_weights, proj_scales):
    n_seqs, n_rows, channels = tokens.shape
    wide_tokens = tokens.astype(jnp.float32)
    mean_square = jnp.mean(wide_tokens * wide_tokens, axis=-1, keepdims=True)
    normed = (wide_tokens * lax.rsqrt(mean_square + 1e-05) * norm_gain).astype(jnp.bfloat16)
    flat_rows = normed.reshape(n_seqs * n_rows, channels)
    in_pair = proj_weights[0:2]
    wide_local = proj_weights.astype(jnp.float32)
    all_squares = lax.psum(jnp.sum(wide_local * wide_local, axis=1), "chan")
    weight_rows = lax.all_gather(in_pair, "chan", axis=1, tiled=True)
    sliced = flat_rows
    value_raw = jnp.dot(sliced, weight_rows[0], preferred_element_type=jnp.float32)
    gate_raw = jnp.dot(sliced, weight_rows[1], preferred_element_type=jnp.float32)
    in_squares = all_squares[0:2]
    value = (
        (value_raw * column_scale(in_squares[0], proj_scales[0]))
        .astype(jnp.bfloat16)
        .reshape(n_seqs, n_rows, channels)
    )
    gate = (gate_raw * column_scale(in_squares[1], proj_scales[1])).astype(jnp.bfloat16)
    first_mix = first_factor(value, block_weights)
    second_mix = jnp.einsum(
        "tab,nbtc->natc",
        stride_weights,
        lax.all_to_all(first_mix, ("ctx", "chan"), split_axis=2, concat_axis=1, tiled=True),
        preferred_element_type=jnp.float32,
    ).astype(jnp.bfloat16)
    returned = lax.all_to_all(second_mix, ("ctx", "chan"), split_axis=1, concat_axis=2, tiled=True)
    mixed = returned.reshape(n_seqs * n_rows, channels)
    hidden = (mixed.astype(jnp.float32) * jax.nn.silu(gate.astype(jnp.float32))).astype(
        jnp.bfloat16
    )
    out_part = proj_weights[2]
    sliced = hidden
    out_raw = jnp.dot(
        sliced,
        lax.all_gather(out_part, "chan", axis=0, tiled=True),
        preferred_element_type=jnp.float32,
    )
    out_squares = all_squares[2]
    result = out_raw * column_scale(out_squares, proj_scales[2])
    return result.astype(jnp.bfloat16).reshape(n_seqs, n_rows, channels)


def solution(mesh):
    placed = (
        P(None, ("ctx", "chan"), None),
        P(),
        P(("ctx", "chan"), None, None),
        P(("ctx", "chan"), None, None),
        P(None, "chan", None),
        P(),
    )
    return jax.shard_map(
        local, mesh=mesh, in_specs=placed, out_specs=P(None, ("ctx", "chan"), None), check_vma=False
    )
```

profile of v0, /device:TPU:0, one launch (start us, length us, event | category | flops | bytes accessed | tf_op | source)
XLA Modules:
  0.0 234.3 jit_solution(10567544898022039140)
XLA Ops:
  6.5 1.9 slice.33
  8.4 0.0 all-gather.4.cloned.1.call-update
  8.4 1.1 multiply_reduce_fusion
  9.5 34.7 %psum.7 = f32[3,768]{1,0:T(4,128)S(1)} all-reduce(f32[3,768]{1,0:T(4,128)S(1)} %multiply_reduce_fusion), channel_id=1, replica_groups=mesh['ctx'=16,'chan'=8] {'chan'}, use_global_device_ids=true, to_apply=%region_2.0 | all-reduce | flops 2304 | bytes 18432 | tf_op jit(solution)/shard_map/psum | solution.py:28
  44.2 0.9 fusion.28
  45.1 2.6 %fusion = f32[2048]{0:T(1024)S(1)} fusion(bf16[1,2048,768]{2,1,0:T(8,128)(2,1)} %param.6), kind=kLoop, calls=%fused_computation.4 | loop fusion | flops 4716544 | bytes 3153920 | tf_op jit(solution)/shard_map/reduce_sum | solution.py:23
  47.7 20.3 %all-gather.4.cloned.1.call-done = bf16[2,768,768]{2,1,0:T(8,128)(2,1)} async-done(((bf16[2,96,768]{2,1,0:T(8,128)(2,1)}), bf16[2,768,768]{2,1,0:T(8,128)(2,1)}) %all-gather.4.cloned.1.call-update) | async-done | bytes 2359312 | tf_op jit(solution)/shard_map/all_gather | solution.py:29
  68.0 4.9 %multiply_convert_fusion.2 = bf16[2048,768]{1,0:T(8,128)(2,1)S(1)} fusion(f32[768]{0:T(1024)S(1)} %get-tuple-element.7, bf16[2,768,768]{2,1,0:T(8,128)(2,1)} %all-gather.4.cloned.1.call-done, bf16[1,2048,768]{2,1,0:T(8,128)(2,1)} %param.6, f32[768]{0:T(1024)S(1)} %copy-done.2, f32[2048]{0:T(1024)S(1)} %add_rsqrt_fusion), kind=kOutput, calls=%fused_computation.14 | convolution fusion | flops 2425356288 | bytes 7485440 | tf_op jit(solution)/shard_map/dot_general | solution.py:31
  73.0 3.8 %convert_bitcast_fusion.2 = bf16[1,4,512,768]{2,3,1,0:T(8,128)(2,1)} fusion(bf16[4,512,768]{2,1,0:T(8,128)(2,1)S(1)} %bitcast.39, bf16[4,512,512]{2,1,0:T(8,128)(2,1)S(1)} %copy-done), kind=kOutput, calls=%fused_computation.20 | convolution fusion | flops 1612185600 | bytes 8388608 | tf_op jit(solution)/shard_map/bts,nbsc->nbtc/dot_general | solution.py:15
  76.7 6.0 %copy.17 = bf16[1,4,512,768]{3,1,0,2:T(4,128)(2,1)} copy(bf16[1,4,512,768]{2,3,1,0:T(8,128)(2,1)} %convert_bitcast_fusion.2) | data formatting | bytes 6291456 | tf_op jit(solution)/shard_map/convert_element_type | solution.py:17
  82.8 51.3 %all_to_all.24 = bf16[1,4,512,768]{3,1,0,2:T(4,128)(2,1)S(1)} all-to-all(bf16[1,4,512,768]{3,1,0,2:T(4,128)(2,1)} %copy.17), channel_id=1, replica_groups=mesh['ctx'=16,'chan'=8] {'ctx','chan'}, dimensions={2} | all-to-all | bytes 6291456 | tf_op jit(solution)/shard_map/all_to_all | solution.py:44
  134.1 1.2 copy.18
  135.3 0.3 copy-done.1
  135.6 3.8 %convert_bitcast_fusion.1 = bf16[1,512,4,768]{1,3,2,0:T(8,128)(2,1)} fusion(bf16[4,512,512]{2,1,0:T(8,128)(2,1)S(1)} %copy-done.1, bf16[512,4,768]{2,1,0:T(4,128)(2,1)S(1)} %bitcast.38), kind=kOutput, calls=%fused_computation.19 | convolution fusion | flops 1612185600 | bytes 8388608 | tf_op jit(solution)/shard_map/tab,nbtc->natc/dot_general | solution.py:41
  139.5 6.0 %copy.20 = bf16[1,512,4,768]{3,2,0,1:T(4,128)(2,1)} copy(bf16[1,512,4,768]{1,3,2,0:T(8,128)(2,1)} %convert_bitcast_fusion.1) | data formatting | bytes 6291456 | tf_op jit(solution)/shard_map/convert_element_type | solution.py:46
  145.5 5.7 %all-to-all-start.1 = ((bf16[1,512,4,768]{3,2,0,1:T(4,128)(2,1)}), bf16[1,512,4,768]{3,2,0,1:T(4,128)(2,1)}, u32[]{:S(2)}, u32[]{:S(2)}) async-start(bf16[1,512,4,768]{3,2,0,1:T(4,128)(2,1)} %copy.20), calls=%async_computation.1 | async-start | bytes 6291456 | tf_op jit(solution)/shard_map/all_to_all | solution.py:47
  151.3 0.2 all-gather.6.cloned.1.call-start
  151.5 1.6 slice.40
  153.1 0.0 all-gather.6.cloned.1.call-update
  153.1 49.0 %all-to-all-done.1 = bf16[1,512,4,768]{3,2,0,1:T(4,128)(2,1)} async-done(((bf16[1,512,4,768]{3,2,0,1:T(4,128)(2,1)}), bf16[1,512,4,768]{3,2,0,1:T(4,128)(2,1)}, u32[]{:S(2)}, u32[]{:S(2)}) %all-to-all-start.1) | async-done | bytes 3145760 | tf_op jit(solution)/shard_map/all_to_all | solution.py:47
  202.1 3.7 %convert_bitcast_fusion = f32[1,4,128,4,768]{4,3,1,2,0:T(4,128)S(1)} fusion(bf16[1,128,4,4,768]{4,3,2,1,0:T(4,128)(2,1)} %bitcast.18), kind=kLoop, calls=%fused_computation.11 | loop fusion | flops 1572864 | bytes 9437184 | tf_op jit(solution)/shard_map/convert_element_type | solution.py:49
  205.8 3.7 %copy.21 = f32[1,4,128,4,768]{4,3,2,1,0:T(4,128)} copy(f32[1,4,128,4,768]{4,3,1,2,0:T(4,128)S(1)} %convert_bitcast_fusion) | data formatting | bytes 12582912 | tf_op jit(solution)/shard_map/convert_element_type | solution.py:49
  209.5 7.7 %reshape.44 = f32[2048,768]{1,0:T(8,128)} reshape(f32[1,4,128,4,768]{4,3,2,1,0:T(4,128)} %copy.21) | data formatting | bytes 12582912 | tf_op jit(solution)/shard_map/convert_element_type | solution.py:49
  217.3 10.1 %fusion.12 = bf16[1,2048,768]{2,1,0:T(8,128)(2,1)} fusion(f32[768]{0:T(1024)S(1)} %get-tuple-element.6, f32[2048,768]{1,0:T(8,128)} %reshape.44, f32[768]{0:T(1024)S(1)} %get-tuple-element.5, bf16[2,768,768]{2,1,0:T(8,128)(2,1)} %all-gather.4.cloned.1.call-done, bf16[1,768,768]{2,1,0:T(8,128)(2,1)} %all-gather.6.cloned.1.call-done, ...), kind=kOutput, calls=%fused_computation.21 | convolution fusion | flops 4855431168 | bytes 14959616 | tf_op jit(solution)/shard_map/dot_general | solution.py:54
  (8 shorter events, 0.0 us)
Async XLA Ops:
  6.5 66.4 %copy-start = (bf16[4,512,512]{2,1,0:T(8,128)(2,1)S(1)}, bf16[4,512,512]{2,1,0:T(8,128)(2,1)}, u32[]{:S(2)}) copy-start(bf16[4,512,512]{2,1,0:T(8,128)(2,1)} %param.8) | copy-start | bytes 6291460
  6.5 61.5 %copy-start.2 = (f32[768]{0:T(1024)S(1)}, f32[768]{0:T(1024)}, u32[]{:S(2)}) copy-start(f32[768]{0:T(1024)} %param.7) | copy-start | bytes 9220
  6.5 61.5 %all-gather.4.cloned.1.call-start = ((), (), s32[]{:S(2)}) async-start(), calls=%async_computation.2 | async-start | bytes 2654208 | tf_op jit(solution)/shard_map/all_gather | solution.py:29
  134.0 1.6 copy-start.1
  145.5 56.5 %all-to-all-start.1 = ((bf16[1,512,4,768]{3,2,0,1:T(4,128)(2,1)}), bf16[1,512,4,768]{3,2,0,1:T(4,128)(2,1)}, u32[]{:S(2)}, u32[]{:S(2)}) async-start(bf16[1,512,4,768]{3,2,0,1:T(4,128)(2,1)} %copy.20), calls=%async_computation.1 | async-start | bytes 6291456 | tf_op jit(solution)/shard_map/all_to_all | solution.py:47
  151.3 66.0 %all-gather.6.cloned.1.call-start = ((), (), s32[]{:S(2)}) async-start(), calls=%async_computation.3 | async-start | bytes 1327104 | tf_op jit(solution)/shard_map/all_gather | solution.py:56
Sparse Core Ops, SparseCore 0:
  9.0 58.9 all-gather.3
  153.7 57.2 all-gather.5
where the time goes:
time: 235 us; the launch traced here: 234 us
  blocking collectives  86 us (37%)
  waiting for transfers between devices  69.3 us (29%)
  local copies, waits for them, and re-layouts  28.6 us (12%)
  matrix products  22.7 us (10%)
  between operations  13.5 us (6%)
  other arithmetic  8.32 us (4%)
  starting transfers between devices  5.96 us (3%)
    all_to_all x1, blocking collectives, local(): lax.all_to_all(first_mix, ('ctx', 'chan'), split_axis=2, concat_axis=1, t...  51.3 us
    all_to_all x1, waiting for transfers between devices, local(): lax.all_to_all(second_mix, ('ctx', 'chan'), split_axis=1, concat_axis=2,...  49 us
    psum x1, blocking collectives, local(): all_squares = lax.psum(jnp.sum(wide_local * wide_local, axis=1), 'chan')  34.7 us
    all_gather x1, waiting for transfers between devices, local(): weight_rows = lax.all_gather(in_pair, 'chan', axis=1, tiled=True)  20.3 us
    convert_element_type x2, local copies, waits for them, and re-layouts, local(): mixed.astype(jnp.float32) * jax.nn.silu(gate.astype(jnp.float32))  11.5 us
    dot_general x1, matrix products, local(): jnp.dot(sliced, lax.all_gather(out_part, 'chan', axis=0, tiled=True), pre...  10.1 us
    convert_element_type x1, local copies, waits for them, and re-layouts, local(): second_mix = jnp.einsum('tab,nbtc->natc', stride_weights, lax.all_to_all(...  6.05 us
    convert_element_type x1, local copies, waits for them, and re-layouts, first_factor(): return jnp.einsum('bts,nbsc->nbtc', block_weights, grouped, preferred_ele...  6.04 us
  transfers between devices with their start and end apart: 3, of which 2 were waited for; matrix products, arithmetic and copies ran while one was open for 9% of the time, Pallas kernels for 0%

commit v1 on v0

v1 whole, which is shorter than its diff:
```python
import functools

import jax
import jax.numpy as jnp
from jax import lax
from jax.experimental import pallas as pl
from jax.experimental.pallas import tpu as pltpu
from jax.sharding import PartitionSpec as P

MESH = pl.DeviceIdType.MESH
ORDERS = ((0, 1, 2), (1, 2, 0), (2, 0, 1)) * 2
CHUNKS = len(ORDERS)
WIDTH = 128
PIECE = 16


def coordinates():
    c, h = lax.axis_index("ctx"), lax.axis_index("chan")
    return h // 2, (c // 8) * 2 + h % 2, (c // 2) % 4, c % 2


def device_at(x, y, z, k):
    return (y // 2) * 8 + z * 2 + k, x * 2 + y % 2


def neighbour(me, offset):
    x, y, z, k = [(m + o) % n for m, o, n in zip(me, offset, (4, 4, 4, 2))]
    return device_at(x, y, z, k)


def along(axis, step, core=0):
    offset = [0, 0, 0, core]
    offset[axis] = step
    return tuple(offset)


PARTNERS = [along(axis, step, core) for axis in range(3) for step in (1, 3, 2) for core in (0, 1)] + [(0, 0, 0, 1)]


def send_slot(order, point):
    a, b, c = order
    return point[a], point[3], point[b], point[c]


def landed_slot(order, point):
    a, b, c = order
    return point[c], point[b], point[a], point[3]


class Journey:
    def __init__(self, me, chunk, buffers, sems, first_sem):
        self.me, self.chunk, self.buffers, self.sems, self.first_sem = me, chunk, buffers, sems, first_sem

    def copies(self, hop):
        me, chunk = self.me, self.chunk
        axis = ORDERS[chunk][hop]
        source, target = self.buffers[hop], self.buffers[hop + 1]
        here = me[axis]
        send_sem, recv_sem = [s.at[self.first_sem + hop] for s in self.sems]
        local, remote = [], []
        for core in (0, 1) if hop == 0 else (0,):
            for step in (0, 1, 3, 2):
                there = (here + step) % 4
                if hop == 0:
                    src = source.at[chunk, there, (me[3] + core) % 2]
                    dst = target.at[chunk, here, me[3]]
                elif hop == 1:
                    src, dst = source.at[chunk, :, :, there], target.at[chunk, here]
                else:
                    src, dst = source.at[chunk, :, :, :, there], target.at[chunk, here]
                offset = along(axis, step, core)
                if offset == (0, 0, 0, 0):
                    local.append((src, dst, recv_sem))
                else:
                    remote.append((src, dst, send_sem, recv_sem, neighbour(me, offset)))
        return local, remote

    def start(self, hop):
        local, remote = self.copies(hop)
        for src, dst, send_sem, recv_sem, device in remote:
            pltpu.make_async_remote_copy(
                src_ref=src, dst_ref=dst, send_sem=send_sem, recv_sem=recv_sem, device_id=device, device_id_type=MESH
            ).start()
        for src, dst, sem in local:
            pltpu.make_async_copy(src, dst, sem).start()


    def wait(self, hop):
        whole = self.buffers[hop + 1].at[self.chunk]
        pltpu.make_async_copy(whole, whole, self.sems[1].at[self.first_sem + hop]).wait()

    def wait_sent(self, hop, rows):
        if hop == 0:
            sent = rows.at[:, pl.ds(0, 448), :]
        else:
            sent = self.buffers[hop].at[self.chunk, pl.ds(0, 3)]
        pltpu.make_async_copy(sent, sent, self.sems[0].at[self.first_sem + hop]).wait()


def each_octet(body):
    def step(m, carry):
        body(m, m // 8, (m // 2) % 4, m % 2)
        return carry

    lax.fori_loop(0, 16, step, 0)


def mix_kernel(
    tokens,
    gain,
    block_w,
    stride_w,
    out,
    normed,
    block_v,
    stride_v,
    wide,
    rows,
    mixed,
    fwd0,
    fwd1,
    fwd2,
    fwd3,
    ret0,
    ret1,
    ret2,
    ret3,
    out_v,
    load_sems,
    out_sems,
    send_sems,
    recv_sems,
):
    me = coordinates()
    sems = (send_sems, recv_sems)
    loads = [pltpu.make_async_copy(tokens.at[b], normed.at[b], load_sems.at[b]) for b in range(4)]
    loads.append(pltpu.make_async_copy(block_w, block_v, load_sems.at[4]))
    loads.append(pltpu.make_async_copy(stride_w, stride_v, load_sems.at[5]))
    for load in loads:
        load.start()
    barrier = pltpu.get_barrier_semaphore()
    for offset in PARTNERS:
        pl.semaphore_signal(barrier, inc=1, device_id=neighbour(me, offset), device_id_type=MESH)

    for b in range(4):
        loads[b].wait()

        def norm(i, carry, b=b):
            r = pl.ds(pl.multiple_of(i * 64, 64), 64)
            x = normed[b, r, :].astype(jnp.float32)
            scale = lax.rsqrt(jnp.mean(x * x, axis=-1, keepdims=True) + 1e-05)
            normed[b, r, :] = (x * scale * gain[...]).astype(jnp.bfloat16)
            return carry

        lax.fori_loop(0, 8, norm, 0)
    loads[4].wait()

    forward = [Journey(me, c, (fwd0, fwd1, fwd2, fwd3), sems, 3 * c) for c in range(CHUNKS)]
    back = [Journey(me, c, (ret0, ret1, ret2, ret3), sems, 3 * (CHUNKS + c)) for c in range(CHUNKS)]

    low = lax.broadcasted_iota(jnp.int32, (8, WIDTH), 0) < 4

    def paired(p, q):
        return jnp.where(low, p, pltpu.roll(q, 4, 0)), jnp.where(low, pltpu.roll(p, 4, 0), q)

    for g in range(CHUNKS // 2):
        for b in range(4):
            x = jnp.dot(block_v[b], normed[b, :, pl.ds(g * 256, 256)], preferred_element_type=jnp.float32)
            for half in range(2):
                wide[half, pl.ds(b, 512, stride=4), :] = x[:, half * WIDTH : (half + 1) * WIDTH]
        for half in range(2):
            chunk = 2 * g + half

            def pack(m, y_hi, z, core, half=half, chunk=chunk):
                for x in range(4):
                    for y_lo in range(2):
                        r = pl.ds(pl.multiple_of((m * 8 + x * 2 + y_lo) * PIECE, PIECE), PIECE)
                        slot = send_slot(ORDERS[chunk], (x, y_hi * 2 + y_lo, z, core))
                        fwd0[(chunk, *slot)] = wide[half, r, :].astype(jnp.bfloat16)

            each_octet(pack)
            if chunk == 0:
                pl.semaphore_wait(barrier, len(PARTNERS))
            forward[chunk].start(0)

    for hop in range(2):
        for chunk in range(CHUNKS):
            forward[chunk].wait(hop)
            forward[chunk].start(hop + 1)
    loads[5].wait()

    for chunk in range(CHUNKS):
        forward[chunk].wait(2)

        def split(m, y_hi, z, core, chunk=chunk):
            per_t = [[] for _ in range(4)]
            for x in range(4):
                even, odd = [
                    fwd3[(chunk, *landed_slot(ORDERS[chunk], (x, y_hi * 2 + y_lo, z, core)))].astype(jnp.float32)
                    for y_lo in range(2)
                ]
                for j in range(2):
                    first, second = paired(even[8 * j : 8 * j + 8], odd[8 * j : 8 * j + 8])
                    per_t[2 * j].append(first)
                    per_t[2 * j + 1].append(second)
            r = pl.ds(pl.multiple_of(m * 32, 32), 32)
            for t in range(4):
                rows[t, r, :] = jnp.concatenate(per_t[t], axis=0).astype(jnp.bfloat16)

        each_octet(split)
        for t in range(4):
            mixed[t] = jnp.dot(stride_v[t], rows[t], preferred_element_type=jnp.float32)

        def join(m, y_hi, z, core, chunk=chunk):
            for x in range(4):
                r = pl.ds(pl.multiple_of(m * 32 + x * 8, 8), 8)
                top = paired(mixed[0, r, :], mixed[1, r, :])
                bottom = paired(mixed[2, r, :], mixed[3, r, :])
                for y_lo in range(2):
                    slot = send_slot(ORDERS[chunk], (x, y_hi * 2 + y_lo, z, core))
                    ret0[(chunk, *slot)] = jnp.concatenate([top[y_lo], bottom[y_lo]], axis=0).astype(jnp.bfloat16)

        each_octet(join)
        back[chunk].start(0)

    for hop in range(2):
        for chunk in range(CHUNKS):
            back[chunk].wait(hop)
            back[chunk].start(hop + 1)

    stores = []
    for chunk in range(CHUNKS):
        back[chunk].wait(2)

        def unpack(m, y_hi, z, core, chunk=chunk):
            for x in range(4):
                for y_lo in range(2):
                    r = pl.ds(pl.multiple_of((m * 8 + x * 2 + y_lo) * PIECE, PIECE), PIECE)
                    slot = landed_slot(ORDERS[chunk], (x, y_hi * 2 + y_lo, z, core))
                    wide[0, r, :] = ret3[(chunk, *slot)].astype(jnp.float32)

        each_octet(unpack)
        for a in range(4):
            out_v[chunk, a] = wide[0, pl.ds(a, 512, stride=4), :].astype(jnp.bfloat16)
        stores.append(
            pltpu.make_async_copy(out_v.at[chunk], out.at[:, :, pl.ds(chunk * WIDTH, WIDTH)], out_sems.at[chunk])
        )
        stores[-1].start()
    for chunk in range(CHUNKS):
        for hop in range(3):
            forward[chunk].wait_sent(hop, rows)
            back[chunk].wait_sent(hop, rows)
    for store in stores:
        store.wait()


def mix(tokens, gain, block_w, stride_w):
    sent = (CHUNKS, 4, 2, 4, 4, PIECE, WIDTH)
    half_way = (CHUNKS, 4, 4, 2, 4, PIECE, WIDTH)
    landed = (CHUNKS, 4, 4, 4, 2, PIECE, WIDTH)
    bf16, f32 = jnp.bfloat16, jnp.float32
    hbm = pl.BlockSpec(memory_space=pl.ANY)
    return pl.pallas_call(
        mix_kernel,
        out_shape=jax.ShapeDtypeStruct((4, 512, 768), bf16),
        in_specs=[hbm, pl.BlockSpec(memory_space=pltpu.VMEM), hbm, hbm],
        out_specs=hbm,
        scratch_shapes=[
            pltpu.VMEM((4, 512, 768), bf16),
            pltpu.VMEM((4, 512, 512), bf16),
            pltpu.VMEM((4, 512, 512), bf16),
            pltpu.VMEM((2, 2048, WIDTH), f32),
            pltpu.VMEM((4, 512, WIDTH), bf16),
            pltpu.VMEM((4, 512, WIDTH), f32),
            *[pltpu.VMEM(s, bf16) for s in (sent, sent, half_way, landed)],
            *[pltpu.VMEM(s, bf16) for s in (sent, sent, half_way, landed)],
            pltpu.VMEM((CHUNKS, 4, 512, WIDTH), bf16),
            pltpu.SemaphoreType.DMA((6,)),
            pltpu.SemaphoreType.DMA((CHUNKS,)),
            *[pltpu.SemaphoreType.DMA((6 * CHUNKS,)) for _ in range(2)],
        ],
        compiler_params=pltpu.CompilerParams(collective_id=0, has_side_effects=True, vmem_limit_bytes=56 << 20),
        cost_estimate=pl.CostEstimate(flops=3 << 30, bytes_accessed=40 << 20, transcendentals=0),
        name="monarch_mix",
    )(tokens, gain, block_w, stride_w)


def local(tokens, norm_gain, block_weights, stride_weights, proj_weights, proj_scales):
    channels = tokens.shape[-1]
    weights = lax.all_gather(proj_weights, "chan", axis=1, tiled=True)
    carried = mix(tokens.reshape(4, 512, channels), norm_gain.reshape(1, channels), block_weights, stride_weights)
    carried = carried.reshape(2048, channels)
    wide_weights = weights.astype(jnp.float32)
    colscale = proj_scales * lax.rsqrt(jnp.sum(wide_weights * wide_weights, axis=1) + 1e-06)
    wide_tokens = tokens.reshape(2048, channels).astype(jnp.float32)
    mean_square = jnp.mean(wide_tokens * wide_tokens, axis=-1, keepdims=True)
    normed = (wide_tokens * lax.rsqrt(mean_square + 1e-05) * norm_gain).astype(jnp.bfloat16)

    def project(rows, k):
        return (jnp.dot(rows, weights[k], preferred_element_type=jnp.float32) * colscale[k]).astype(jnp.bfloat16)

    gate = project(normed, 1).astype(jnp.float32)
    mixed = project(carried, 0).astype(jnp.float32)
    hidden = (mixed * jax.nn.silu(gate)).astype(jnp.bfloat16)
    return project(hidden, 2).reshape(tokens.shape)


def solution(mesh):
    placed = (
        P(None, ("ctx", "chan"), None),
        P(),
        P(("ctx", "chan"), None, None),
        P(("ctx", "chan"), None, None),
        P(None, "chan", None),
        P(),
    )
    return jax.shard_map(
        local, mesh=mesh, in_specs=placed, out_specs=P(None, ("ctx", "chan"), None), check_vma=False
    )
```

time: 235 us -> 185 us (0.79)
  Pallas kernels: 0 us -> 148 us
  blocking collectives: 86 us -> 0 us
  waiting for transfers between devices: 69.3 us -> 0.73 us
  local copies, waits for them, and re-layouts: 28.6 us -> 1.44 us
  matrix products: 22.7 us -> 15 us
  starting transfers between devices: 5.96 us -> 0.01 us
    pallas_call x0 -> x1, Pallas kernels: none -> 148 us  [mix(): pl.pallas_call(mix_kernel, out_shape=jax.ShapeDtypeStruct((4, 512, 768),...]
    all_to_all x1 -> x0, blocking collectives: 51.3 us -> none  [local(): lax.all_to_all(first_mix, ('ctx', 'chan'), split_axis=2, concat_axis=1, t...]
    all_to_all x1 -> x0, waiting for transfers between devices: 49 us -> none  [local(): lax.all_to_all(second_mix, ('ctx', 'chan'), split_axis=1, concat_axis=2,...]
    psum x1 -> x0, blocking collectives: 34.7 us -> none  [local(): all_squares = lax.psum(jnp.sum(wide_local * wide_local, axis=1), 'chan')]
    convert_element_type x4 -> x0, local copies, waits for them, and re-layouts: 23.6 us -> none  [the longest x2 11.5 us: local(): mixed.astype(jnp.float32) * jax.nn.silu(gate.astype(jnp.float32))]
    all_gather x2 -> x1, waiting for transfers between devices: 20.3 us -> 0.02 us  [local(): weights = lax.all_gather(proj_weights, 'chan', axis=1, tiled=True)]
    dot_general x4 -> x2, matrix products: 22.7 us -> 15 us  [project(): jnp.dot(rows, weights[k], preferred_element_type=jnp.float32) * colscale[k]]
    all_to_all x1 -> x0, starting transfers between devices: 5.73 us -> none  [local(): lax.all_to_all(second_mix, ('ctx', 'chan'), split_axis=1, concat_axis=2,...]
  transfers between devices with their start and end apart: 3 -> 1, of which waited for: 2 -> 0; matrix products, arithmetic and copies ran while one was open for 9% -> 2% of each run, Pallas kernels for 0% -> 80%
where the time goes in v1:
time: 185 us
  Pallas kernels  148 us (80%)
  matrix products  15 us (8%)
  between operations  13.5 us (7%)
  other arithmetic  6.06 us (3%)
    pallas_call x1, Pallas kernels, mix(): pl.pallas_call(mix_kernel, out_shape=jax.ShapeDtypeStruct((4, 512, 768),...  148 us
    dot_general x2, matrix products, project(): jnp.dot(rows, weights[k], preferred_element_type=jnp.float32) * colscale[k]  15 us
  transfers between devices with their start and end apart: 1, of which 0 were waited for; matrix products, arithmetic and copies ran while one was open for 2% of the time, Pallas kernels for 80%

profile of v1, /device:TPU:0, one launch (start us, length us, event | category | flops | bytes accessed | tf_op | source)
XLA Modules:
  0.0 184.6 jit_solution(2586584858595678743)
XLA Ops:
  6.5 0.0 all-gather.2.cloned.1.call-start
  6.5 0.7 all-gather.2.cloned.1.call-update
  7.3 1.3 reshape.39.gain
  8.5 2.6 %fusion = f32[2048]{0:T(1024)S(1)} fusion(bf16[1,2048,768]{2,1,0:T(8,128)(2,1)} %param.6), kind=kLoop, calls=%fused_computation.5 | loop fusion | flops 4716544 | bytes 3153920 | tf_op jit(solution)/shard_map/reduce_sum | solution.py:296
  11.1 0.6 add_rsqrt_fusion
  11.7 147.9 %monarch_mix.1 = bf16[4,512,768]{2,1,0:T(8,128)(2,1)} custom-call(bf16[4,512,768]{2,1,0:T(8,128)(2,1)} %bitcast.18, f32[1,768]{1,0:T(1,128)} %reshape.39.gain, bf16[4,512,512]{2,1,0:T(8,128)(2,1)} %block_w.1, bf16[4,512,512]{2,1,0:T(8,128)(2,1)} %stride_w.1), custom_call_target="tpu_custom_call" | custom-call | flops 3221225472 | bytes 41943040 | tf_op jit(solution)/shard_map/monarch_mix/pallas_call | solution.py:263
  159.6 0.0 copy-start.1
  159.6 0.0 copy-start.3
  159.6 0.0 all-gather.2.cloned.1.call-done
  159.7 0.0 copy-start
  159.7 0.0 copy-start.2
  159.7 2.9 %multiply_reduce_fusion = f32[3,768]{1,0:T(4,128)S(1)} fusion(bf16[3,768,768]{2,1,0:T(8,128)(2,1)} %all-gather.2.cloned.1.call-done), kind=kLoop, calls=%fused_computation.4 | loop fusion | flops 5306112 | bytes 3548160 | tf_op jit(solution)/shard_map/reduce_sum | solution.py:294
  162.5 0.0 copy-done.1
  162.6 0.0 copy-done.3
  162.6 0.1 copy-done
  162.7 0.0 copy-done.2
  162.7 6.3 %multiply_convert_fusion.1 = bf16[2048,768]{1,0:T(8,128)(2,1)} fusion(bf16[1,2048,768]{2,1,0:T(8,128)(2,1)} %param.6, f32[768]{0:T(1024)S(1)} %get-tuple-element.7, f32[768]{0:T(1024)S(1)} %copy-done.3, f32[2048]{0:T(1024)S(1)} %copy-done.2, bf16[3,768,768]{2,1,0:T(8,128)(2,1)S(1)} %copy-done), kind=kOutput, calls=%fused_computation.13 | convolution fusion | flops 2425356288 | bytes 7487488 | tf_op jit(solution)/shard_map/dot_general | solution.py:300
  169.0 8.7 %fusion.13 = bf16[1,2048,768]{2,1,0:T(8,128)(2,1)} fusion(f32[768]{0:T(1024)S(1)} %get-tuple-element.6, bf16[2048,768]{1,0:T(8,128)(2,1)} %multiply_convert_fusion.1, bf16[2048,768]{1,0:T(8,128)(2,1)} %bitcast.19, f32[768]{0:T(1024)S(1)} %get-tuple-element.5, bf16[3,768,768]{2,1,0:T(8,128)(2,1)S(1)} %copy-done), kind=kOutput, calls=%fused_computation.19 | convolution fusion | flops 4850712576 | bytes 11804672 | tf_op jit(solution)/shard_map/dot_general | solution.py:300
  (2 shorter events, 0.0 us)
Async XLA Ops:
  6.5 153.1 %all-gather.2.cloned.1.call-start = ((), (), s32[]{:S(2)}) async-start(), calls=%async_computation | async-start | bytes 3981312 | tf_op jit(solution)/shard_map/all_gather | solution.py:290
  159.6 2.9 %copy-start.1 = (f32[3,768]{1,0:T(4,128)S(1)}, f32[3,768]{1,0:T(4,128)}, u32[]{:S(2)}) copy-start(f32[3,768]{1,0:T(4,128)} %param.11) | copy-start | bytes 27652
  159.6 3.0 %copy-start.3 = (f32[768]{0:T(1024)S(1)}, f32[768]{0:T(1024)}, u32[]{:S(2)}) copy-start(f32[768]{0:T(1024)} %param.7) | copy-start | bytes 9220
  159.7 3.1 %copy-start = (bf16[3,768,768]{2,1,0:T(8,128)(2,1)S(1)}, bf16[3,768,768]{2,1,0:T(8,128)(2,1)}, u32[]{:S(2)}) copy-start(bf16[3,768,768]{2,1,0:T(8,128)(2,1)} %all-gather.2.cloned.1.call-done) | copy-start | bytes 10616836
  159.7 3.1 %copy-start.2 = (f32[2048]{0:T(1024)S(1)}, f32[2048]{0:T(1024)}, u32[]{:S(2)}) copy-start(f32[2048]{0:T(1024)} %add_rsqrt_fusion) | copy-start | bytes 24580
Sparse Core Ops, SparseCore 0:
  9.0 113.0 all-gather.1

commit v2 on v1

--- a/solution.py
+++ b/solution.py
@@ -97,6 +97,64 @@
         pltpu.make_async_copy(sent, sent, self.sems[0].at[self.first_sem + hop]).wait()
 
 
+class Gather:
+    def __init__(self, me, proj_w, weights, send_sems, recv_sems):
+        self.me, self.proj_w, self.weights, self.send_sems, self.recv_sems = me, proj_w, weights, send_sems, recv_sems
+        self.x, self.y_lo = me[0], me[1] % 2
+        self.mine = self.x * 2 + self.y_lo
+        self.columns = pl.ds(pl.multiple_of(me[3] * 384, 128), 384)
+
+    def shard(self, h, first=0, rows=96):
+        return self.weights.at[:, pl.ds(pl.multiple_of(h * 96 + first, PIECE), rows), :]
+
+    def part(self, h, first=0, rows=96):
+        return self.weights.at[:, pl.ds(pl.multiple_of(h * 96 + first, PIECE), rows), self.columns]
+
+    def copies(self, hop):
+        me, x = self.me, self.x
+        half = (me[2] % 2) * 48
+        if hop == 0:
+            for first, step in ((0, 1), (48, 3)):
+                yield self.proj_w.at[:, pl.ds(first, 48), self.columns], self.part(self.mine, first, 48), along(1, step)
+        elif hop == 1:
+            for step in (1, 3, 2):
+                for y_lo in range(2):
+                    ref = self.part(x * 2 + y_lo, half, 48)
+                    yield ref, ref, along(0, step)
+        elif hop == 2:
+            for other in (1, 2, 3):
+                for y_lo, step in ((0, 1), (1, 3)):
+                    ref = self.part(((x + other) % 4) * 2 + y_lo, half, 48)
+                    yield ref, ref, along(2, step)
+        else:
+            ref = self.part(x * 2 + 1 - self.y_lo)
+            yield ref, ref, (0, 0, 0, 1)
+            for other in (1, 2, 3):
+                ref = self.part(((x + other) % 4) * 2, 0, 192)
+                yield ref, ref, (0, 0, 0, 1)
+
+    def start(self, hop):
+        for src, dst, offset in self.copies(hop):
+            pltpu.make_async_remote_copy(
+                src_ref=src,
+                dst_ref=dst,
+                send_sem=self.send_sems.at[hop],
+                recv_sem=self.recv_sems.at[hop],
+                device_id=neighbour(self.me, offset),
+                device_id_type=MESH,
+            ).start()
+
+    def _wait(self, sems, hop):
+        ref = self.weights.at[:, pl.ds(0, (96, 288, 288, 672)[hop]), pl.ds(0, 384)]
+        pltpu.make_async_copy(ref, ref, sems.at[hop]).wait()
+
+    def wait(self, hop):
+        self._wait(self.recv_sems, hop)
+
+    def wait_sent(self, hop):
+        self._wait(self.send_sems, hop)
+
+
 def each_octet(body):
     def step(m, carry):
         body(m, m // 8, (m // 2) % 4, m % 2)
@@ -110,13 +168,20 @@
     gain,
     block_w,
     stride_w,
+    proj_w,
+    scales,
     out,
+    out_proj,
+    out_scale,
     normed,
     block_v,
     stride_v,
+    weights,
+    colscale,
     wide,
     rows,
     mixed,
+    total,
     fwd0,
     fwd1,
     fwd2,
@@ -125,17 +190,20 @@
     ret1,
     ret2,
     ret3,
-    out_v,
     load_sems,
     out_sems,
     send_sems,
     recv_sems,
+    gather_send,
+    gather_recv,
 ):
     me = coordinates()
     sems = (send_sems, recv_sems)
     loads = [pltpu.make_async_copy(tokens.at[b], normed.at[b], load_sems.at[b]) for b in range(4)]
     loads.append(pltpu.make_async_copy(block_w, block_v, load_sems.at[4]))
     loads.append(pltpu.make_async_copy(stride_w, stride_v, load_sems.at[5]))
+    gather = Gather(me, proj_w, weights, gather_send, gather_recv)
+    loads.append(pltpu.make_async_copy(proj_w, gather.shard(gather.mine), load_sems.at[6]))
     for load in loads:
         load.start()
     barrier = pltpu.get_barrier_semaphore()
@@ -149,10 +217,12 @@
             r = pl.ds(pl.multiple_of(i * 64, 64), 64)
             x = normed[b, r, :].astype(jnp.float32)
             scale = lax.rsqrt(jnp.mean(x * x, axis=-1, keepdims=True) + 1e-05)
-            normed[b, r, :] = (x * scale * gain[...]).astype(jnp.bfloat16)
+            normed[b, r, :] = (x * scale * gain[...][None, :]).astype(jnp.bfloat16)
             return carry
 
         lax.fori_loop(0, 8, norm, 0)
+    pl.semaphore_wait(barrier, len(PARTNERS))
+    gather.start(0)
     loads[4].wait()
 
     forward = [Journey(me, c, (fwd0, fwd1, fwd2, fwd3), sems, 3 * c) for c in range(CHUNKS)]
@@ -179,15 +249,18 @@
                         fwd0[(chunk, *slot)] = wide[half, r, :].astype(jnp.bfloat16)
 
             each_octet(pack)
-            if chunk == 0:
-                pl.semaphore_wait(barrier, len(PARTNERS))
             forward[chunk].start(0)
 
+    loads[6].wait()
     for hop in range(2):
+        gather.wait(hop)
+        gather.start(hop + 1)
         for chunk in range(CHUNKS):
             forward[chunk].wait(hop)
             forward[chunk].start(hop + 1)
     loads[5].wait()
+    gather.wait(2)
+    gather.start(3)
 
     for chunk in range(CHUNKS):
         forward[chunk].wait(2)
@@ -223,86 +296,143 @@
         each_octet(join)
         back[chunk].start(0)
 
+    gather.wait(3)
+    for k in range(3):
+
+        def add_squares(i, sums, k=k):
+            w = weights[k, pl.ds(pl.multiple_of(i * 64, 64), 64), :].astype(jnp.float32)
+            return sums + jnp.sum((w * w).reshape(8, 8, 768), axis=0)
+
+        sums = lax.fori_loop(0, 12, add_squares, jnp.zeros((8, 768), jnp.float32))
+        squares = jnp.sum(sums, axis=0, keepdims=True)
+        colscale[pl.ds(k, 1), :] = scales[pl.ds(k, 1), :] * lax.rsqrt(squares + 1e-06)
+    out_scale[...] = colscale[pl.ds(2, 1), :]
+    stores = [pltpu.make_async_copy(weights.at[2], out_proj, out_sems.at[8])]
+    stores[0].start()
+
+    def gate_block(i):
+        r = pl.ds((i % 2) * 256, 256)
+        gate = jnp.dot(normed[i // 2, r, :], weights[1], preferred_element_type=jnp.float32)
+        gate = (gate * colscale[pl.ds(1, 1), :]).astype(jnp.bfloat16).astype(jnp.float32)
+        gate = gate / (1.0 + jnp.exp(-gate)) * colscale[pl.ds(0, 1), :]
+        normed[i // 2, r, :] = gate.astype(jnp.bfloat16)
+
     for hop in range(2):
         for chunk in range(CHUNKS):
             back[chunk].wait(hop)
             back[chunk].start(hop + 1)
-
-    stores = []
+            if hop * CHUNKS + chunk < 8:
+                gate_block(hop * CHUNKS + chunk)
+
     for chunk in range(CHUNKS):
         back[chunk].wait(2)
 
         def unpack(m, y_hi, z, core, chunk=chunk):
             for x in range(4):
                 for y_lo in range(2):
-                    r = pl.ds(pl.multiple_of((m * 8 + x * 2 + y_lo) * PIECE, PIECE), PIECE)
+                    r = pl.ds(pl.multiple_of((m % 4) * 128 + (x * 2 + y_lo) * PIECE, PIECE), PIECE)
                     slot = landed_slot(ORDERS[chunk], (x, y_hi * 2 + y_lo, z, core))
-                    wide[0, r, :] = ret3[(chunk, *slot)].astype(jnp.float32)
+                    rows[m // 4, r, :] = ret3[(chunk, *slot)]
 
         each_octet(unpack)
-        for a in range(4):
-            out_v[chunk, a] = wide[0, pl.ds(a, 512, stride=4), :].astype(jnp.bfloat16)
-        stores.append(
-            pltpu.make_async_copy(out_v.at[chunk], out.at[:, :, pl.ds(chunk * WIDTH, WIDTH)], out_sems.at[chunk])
-        )
+
+        def project(i, carry, chunk=chunk):
+            left = rows[i // 2, pl.ds(pl.multiple_of((i % 2) * 256, 256), 256), :]
+            right = weights[0, pl.ds(chunk * WIDTH, WIDTH), :]
+            part = jnp.dot(left, right, preferred_element_type=jnp.float32)
+            r = pl.ds(pl.multiple_of(i * 256, 256), 256)
+            for n in range(CHUNKS):
+                piece = part[:, n * WIDTH : (n + 1) * WIDTH]
+                total[n, r, :] = piece if chunk == 0 else total[n, r, :] + piece
+            return carry
+
+        if chunk < CHUNKS - 1:
+            lax.fori_loop(0, 8, project, 0)
+    for i in range(8):
+        project(i, 0)
+        t = pl.ds(i * 64, 64)
+        for n in range(CHUNKS):
+            c = pl.ds(n * WIDTH, WIDTH)
+            for a in range(4):
+                value = total[n, pl.ds(i * 256 + a, 64, stride=4), :]
+                normed[a, t, c] = (value * normed[a, t, c].astype(jnp.float32)).astype(jnp.bfloat16)
+        stores.append(pltpu.make_async_copy(normed.at[:, t, :], out.at[:, t, :], out_sems.at[i]))
         stores[-1].start()
     for chunk in range(CHUNKS):
         for hop in range(3):
             forward[chunk].wait_sent(hop, rows)
             back[chunk].wait_sent(hop, rows)
+    for hop in range(4):
+        gather.wait_sent(hop)
     for store in stores:
         store.wait()
 
 
-def mix(tokens, gain, block_w, stride_w):
+def mix(tokens, gain, block_w, stride_w, proj_w, scales):
     sent = (CHUNKS, 4, 2, 4, 4, PIECE, WIDTH)
     half_way = (CHUNKS, 4, 4, 2, 4, PIECE, WIDTH)
     landed = (CHUNKS, 4, 4, 4, 2, PIECE, WIDTH)
     bf16, f32 = jnp.bfloat16, jnp.float32
-    hbm = pl.BlockSpec(memory_space=pl.ANY)
+    hbm, vmem = pl.BlockSpec(memory_space=pl.ANY), pl.BlockSpec(memory_space=pltpu.VMEM)
     return pl.pallas_call(
         mix_kernel,
-        out_shape=jax.ShapeDtypeStruct((4, 512, 768), bf16),
-        in_specs=[hbm, pl.BlockSpec(memory_space=pltpu.VMEM), hbm, hbm],
-        out_specs=hbm,
+        out_shape=[
+            jax.ShapeDtypeStruct((4, 512, 768), bf16),
+            jax.ShapeDtypeStruct((768, 768), bf16),
+            jax.ShapeDtypeStruct((1, 768), f32),
+        ],
+        in_specs=[hbm, vmem, hbm, hbm, hbm, vmem],
+        out_specs=[hbm, hbm, vmem],
         scratch_shapes=[
             pltpu.VMEM((4, 512, 768), bf16),
             pltpu.VMEM((4, 512, 512), bf16),
             pltpu.VMEM((4, 512, 512), bf16),
+            pltpu.VMEM((3, 768, 768), bf16),
+            pltpu.VMEM((3, 768), f32),
             pltpu.VMEM((2, 2048, WIDTH), f32),
             pltpu.VMEM((4, 512, WIDTH), bf16),
             pltpu.VMEM((4, 512, WIDTH), f32),
+            pltpu.VMEM((CHUNKS, 2048, WIDTH), f32),
             *[pltpu.VMEM(s, bf16) for s in (sent, sent, half_way, landed)],
             *[pltpu.VMEM(s, bf16) for s in (sent, sent, half_way, landed)],
-            pltpu.VMEM((CHUNKS, 4, 512, WIDTH), bf16),
-            pltpu.SemaphoreType.DMA((6,)),
-            pltpu.SemaphoreType.DMA((CHUNKS,)),
+            pltpu.SemaphoreType.DMA((7,)),
+            pltpu.SemaphoreType.DMA((9,)),
             *[pltpu.SemaphoreType.DMA((6 * CHUNKS,)) for _ in range(2)],
+            *[pltpu.SemaphoreType.DMA((4,)) for _ in range(2)],
         ],
         compiler_params=pltpu.CompilerParams(collective_id=0, has_side_effects=True, vmem_limit_bytes=56 << 20),
-        cost_estimate=pl.CostEstimate(flops=3 << 30, bytes_accessed=40 << 20, transcendentals=0),
         name="monarch_mix",
-    )(tokens, gain, block_w, stride_w)
+    )(tokens, gain, block_w, stride_w, proj_w, scales)
+
+
+def project_kernel(hidden, weight, scale, out):
+    product = jnp.dot(hidden[...], weight[...], preferred_element_type=jnp.float32)
+    out[...] = (product * scale[...]).astype(jnp.bfloat16)
+
+
+def project_out(hidden, weight, scale):
+    n, channels = hidden.shape
+    return pl.pallas_call(
+        project_kernel,
+        grid=(n // 256,),
+        out_shape=jax.ShapeDtypeStruct((n, channels), jnp.bfloat16),
+        in_specs=[
+            pl.BlockSpec((256, channels), lambda i: (i, 0)),
+            pl.BlockSpec((channels, channels), lambda i: (0, 0)),
+            pl.BlockSpec((1, channels), lambda i: (0, 0)),
+        ],
+        out_specs=pl.BlockSpec((256, channels), lambda i: (i, 0)),
+        compiler_params=pltpu.CompilerParams(vmem_limit_bytes=32 << 20),
+        name="project_out",
+    )(hidden, weight, scale)
 
 
 def local(tokens, norm_gain, block_weights, stride_weights, proj_weights, proj_scales):
     channels = tokens.shape[-1]
-    weights = lax.all_gather(proj_weights, "chan", axis=1, tiled=True)
-    carried = mix(tokens.reshape(4, 512, channels), norm_gain.reshape(1, channels), block_weights, stride_weights)
-    carried = carried.reshape(2048, channels)
-    wide_weights = weights.astype(jnp.float32)
-    colscale = proj_scales * lax.rsqrt(jnp.sum(wide_weights * wide_weights, axis=1) + 1e-06)
-    wide_tokens = tokens.reshape(2048, channels).astype(jnp.float32)
-    mean_square = jnp.mean(wide_tokens * wide_tokens, axis=-1, keepdims=True)
-    normed = (wide_tokens * lax.rsqrt(mean_square + 1e-05) * norm_gain).astype(jnp.bfloat16)
-
-    def project(rows, k):
-        return (jnp.dot(rows, weights[k], preferred_element_type=jnp.float32) * colscale[k]).astype(jnp.bfloat16)
-
-    gate = project(normed, 1).astype(jnp.float32)
-    mixed = project(carried, 0).astype(jnp.float32)
-    hidden = (mixed * jax.nn.silu(gate)).astype(jnp.bfloat16)
-    return project(hidden, 2).reshape(tokens.shape)
+    hidden, out_weight, out_scale = mix(
+        tokens.reshape(4, 512, channels), norm_gain, block_weights, stride_weights, proj_weights, proj_scales
+    )
+    return project_out(hidden.reshape(2048, channels), out_weight, out_scale).reshape(tokens.shape)
 
 
 def solution(mesh):

time: 185 us -> 110 us (0.59)
  Pallas kernels: 148 us -> 106 us
  matrix products: 15 us -> 0 us
  between operations: 13.5 us -> 0.02 us
  other arithmetic: 6.06 us -> 0 us
  local copies, waits for them, and re-layouts: 1.44 us -> 3.83 us
    pallas_call x1 -> x2, Pallas kernels: 148 us -> 106 us  [the longest x1 101 us: mix(): pl.pallas_call(mix_kernel, out_shape=[jax.ShapeDtypeStruct((4, 512, 768),...]
    dot_general x2 -> x0, matrix products: 15 us -> none  [project(): jnp.dot(rows, weights[k], preferred_element_type=jnp.float32) * colscale[k]]
    reduce_sum x2 -> x0, other arithmetic: 5.43 us -> none  [the longest x1 2.86 us: local(): jnp.sum(wide_weights * wide_weights, axis=1) + 1e-06]
    unnamed x8 -> x6, local copies, waits for them, and re-layouts: 0.13 us -> 3.83 us
  transfers between devices with their start and end apart: 1 -> 0, of which waited for: 0 -> 0; matrix products, arithmetic and copies ran while one was open for 2% -> 0% of each run, Pallas kernels for 80% -> 0%
where the time goes in v2:
time: 110 us
  Pallas kernels  106 us (96%)
  local copies, waits for them, and re-layouts  3.83 us (3%)
    pallas_call x1, Pallas kernels, mix(): pl.pallas_call(mix_kernel, out_shape=[jax.ShapeDtypeStruct((4, 512, 768),...  101 us
    pallas_call x1, Pallas kernels, project_out(): pl.pallas_call(project_kernel, grid=(n // 256,), out_shape=jax.ShapeDtype...  5.39 us
    unnamed x6, local copies, waits for them, and re-layouts  3.83 us

profile of v2, /device:TPU:0, one launch (start us, length us, event | category | flops | bytes accessed | tf_op | source)
XLA Modules:
  0.0 110.0 jit_solution(9516715475694740968)
XLA Ops:
  0.0 100.7 %monarch_mix.1 = (bf16[4,512,768]{2,1,0:T(8,128)(2,1)}, bf16[768,768]{1,0:T(8,128)(2,1)}, f32[1,768]{1,0:T(1,128)}) custom-call(bf16[4,512,768]{2,1,0:T(8,128)(2,1)} %bitcast.4, f32[768]{0:T(1024)} %gain.1, bf16[4,512,512]{2,1,0:T(8,128)(2,1)} %block_w.1, bf16[4,512,512]{2,1,0:T(8,128)(2,1)} %stride_w.1, bf16[3,96,768]{2,1,0:T(8,128)(2,1)} %proj_w.1, ...), custom_call_target="tpu_custom_call" | custom-call | tf_op jit(solution)/shard_map/monarch_mix/pallas_call | solution.py:377
  100.7 0.0 copy-start
  100.7 1.9 %copy-done = bf16[4,512,768]{2,1,0:T(8,128)(2,1)S(1)} copy-done((bf16[4,512,768]{2,1,0:T(8,128)(2,1)S(1)}, bf16[4,512,768]{2,1,0:T(8,128)(2,1)}, u32[]{:S(2)}) %copy-start) | copy-done | bytes 3145752
  102.6 0.0 copy-start.1
  102.6 1.3 %copy-done.1 = bf16[768,768]{1,0:T(8,128)(2,1)S(1)} copy-done((bf16[768,768]{1,0:T(8,128)(2,1)S(1)}, bf16[768,768]{1,0:T(8,128)(2,1)}, u32[]{:S(2)}) %copy-start.1) | copy-done | bytes 1179672
  103.9 0.0 copy-start.2
  103.9 0.7 copy-done.2
  104.6 5.4 %project_out.1 = bf16[2048,768]{1,0:T(8,128)(2,1)} custom-call(bf16[2048,768]{1,0:T(8,128)(2,1)S(1)} %bitcast.3, bf16[768,768]{1,0:T(8,128)(2,1)S(1)} %copy-done.1, f32[1,768]{1,0:T(1,128)S(1)} %copy-done.2), custom_call_target="tpu_custom_call" | custom-call | tf_op jit(solution)/shard_map/project_out/pallas_call | solution.py:415
Async XLA Ops:
  100.7 1.9 %copy-start = (bf16[4,512,768]{2,1,0:T(8,128)(2,1)S(1)}, bf16[4,512,768]{2,1,0:T(8,128)(2,1)}, u32[]{:S(2)}) copy-start(bf16[4,512,768]{2,1,0:T(8,128)(2,1)} %get-tuple-element.8) | copy-start | bytes 9437188
  102.6 1.3 %copy-start.1 = (bf16[768,768]{1,0:T(8,128)(2,1)S(1)}, bf16[768,768]{1,0:T(8,128)(2,1)}, u32[]{:S(2)}) copy-start(bf16[768,768]{1,0:T(8,128)(2,1)} %get-tuple-element.9.weight) | copy-start | bytes 3538948
  103.9 0.7 copy-start.2

commit v3 on v2

--- a/solution.py
+++ b/solution.py
@@ -117,11 +117,15 @@
             for first, step in ((0, 1), (48, 3)):
                 yield self.proj_w.at[:, pl.ds(first, 48), self.columns], self.part(self.mine, first, 48), along(1, step)
         elif hop == 1:
-            for step in (1, 3, 2):
+            for step in (1, 3):
                 for y_lo in range(2):
                     ref = self.part(x * 2 + y_lo, half, 48)
                     yield ref, ref, along(0, step)
         elif hop == 2:
+            for y_lo, step in ((0, 1), (1, 3)):
+                ref = self.part(((x + 4 - step) % 4) * 2 + y_lo, half, 48)
+                yield ref, ref, along(0, step)
+        elif hop == 3:
             for other in (1, 2, 3):
                 for y_lo, step in ((0, 1), (1, 3)):
                     ref = self.part(((x + other) % 4) * 2 + y_lo, half, 48)
@@ -145,7 +149,7 @@
             ).start()
 
     def _wait(self, sems, hop):
-        ref = self.weights.at[:, pl.ds(0, (96, 288, 288, 672)[hop]), pl.ds(0, 384)]
+        ref = self.weights.at[:, pl.ds(0, (96, 192, 96, 288, 672)[hop]), pl.ds(0, 384)]
         pltpu.make_async_copy(ref, ref, sems.at[hop]).wait()
 
     def wait(self, hop):
@@ -181,6 +185,7 @@
     wide,
     rows,
     mixed,
+    carried,
     total,
     fwd0,
     fwd1,
@@ -252,15 +257,15 @@
             forward[chunk].start(0)
 
     loads[6].wait()
+    gather.wait(0)
+    gather.start(1)
     for hop in range(2):
-        gather.wait(hop)
-        gather.start(hop + 1)
         for chunk in range(CHUNKS):
             forward[chunk].wait(hop)
             forward[chunk].start(hop + 1)
+        gather.wait(hop + 1)
+        gather.start(hop + 2)
     loads[5].wait()
-    gather.wait(2)
-    gather.start(3)
 
     for chunk in range(CHUNKS):
         forward[chunk].wait(2)
@@ -297,6 +302,11 @@
         back[chunk].start(0)
 
     gather.wait(3)
+    gather.start(4)
+    for chunk in range(CHUNKS):
+        back[chunk].wait(0)
+        back[chunk].start(1)
+    gather.wait(4)
     for k in range(3):
 
         def add_squares(i, sums, k=k):
@@ -307,7 +317,7 @@
         squares = jnp.sum(sums, axis=0, keepdims=True)
         colscale[pl.ds(k, 1), :] = scales[pl.ds(k, 1), :] * lax.rsqrt(squares + 1e-06)
     out_scale[...] = colscale[pl.ds(2, 1), :]
-    stores = [pltpu.make_async_copy(weights.at[2], out_proj, out_sems.at[8])]
+    stores = [pltpu.make_async_copy(weights.at[2], out_proj, out_sems.at[4])]
     stores[0].start()
 
     def gate_block(i):
@@ -317,12 +327,11 @@
         gate = gate / (1.0 + jnp.exp(-gate)) * colscale[pl.ds(0, 1), :]
         normed[i // 2, r, :] = gate.astype(jnp.bfloat16)
 
-    for hop in range(2):
-        for chunk in range(CHUNKS):
-            back[chunk].wait(hop)
-            back[chunk].start(hop + 1)
-            if hop * CHUNKS + chunk < 8:
-                gate_block(hop * CHUNKS + chunk)
+    for chunk in range(CHUNKS):
+        back[chunk].wait(1)
+        back[chunk].start(2)
+        for i in ((0, 1), (2, 3), (4,), (5,), (6,), (7,))[chunk]:
+            gate_block(i)
 
     for chunk in range(CHUNKS):
         back[chunk].wait(2)
@@ -330,39 +339,34 @@
         def unpack(m, y_hi, z, core, chunk=chunk):
             for x in range(4):
                 for y_lo in range(2):
-                    r = pl.ds(pl.multiple_of((m % 4) * 128 + (x * 2 + y_lo) * PIECE, PIECE), PIECE)
+                    r = pl.ds(pl.multiple_of((m * 8 + x * 2 + y_lo) * PIECE, PIECE), PIECE)
                     slot = landed_slot(ORDERS[chunk], (x, y_hi * 2 + y_lo, z, core))
-                    rows[m // 4, r, :] = ret3[(chunk, *slot)]
+                    wide[chunk % 2, r, :] = ret3[(chunk, *slot)].astype(jnp.float32)
 
         each_octet(unpack)
-
-        def project(i, carry, chunk=chunk):
-            left = rows[i // 2, pl.ds(pl.multiple_of((i % 2) * 256, 256), 256), :]
-            right = weights[0, pl.ds(chunk * WIDTH, WIDTH), :]
-            part = jnp.dot(left, right, preferred_element_type=jnp.float32)
-            r = pl.ds(pl.multiple_of(i * 256, 256), 256)
-            for n in range(CHUNKS):
-                piece = part[:, n * WIDTH : (n + 1) * WIDTH]
-                total[n, r, :] = piece if chunk == 0 else total[n, r, :] + piece
-            return carry
-
-        if chunk < CHUNKS - 1:
-            lax.fori_loop(0, 8, project, 0)
-    for i in range(8):
-        project(i, 0)
-        t = pl.ds(i * 64, 64)
-        for n in range(CHUNKS):
-            c = pl.ds(n * WIDTH, WIDTH)
-            for a in range(4):
-                value = total[n, pl.ds(i * 256 + a, 64, stride=4), :]
-                normed[a, t, c] = (value * normed[a, t, c].astype(jnp.float32)).astype(jnp.bfloat16)
-        stores.append(pltpu.make_async_copy(normed.at[:, t, :], out.at[:, t, :], out_sems.at[i]))
-        stores[-1].start()
+        for a in range(4):
+            part = wide[chunk % 2, pl.ds(a, 512, stride=4), :].astype(jnp.bfloat16)
+            carried[a, :, pl.ds(chunk % 2 * WIDTH, WIDTH)] = part
+        if chunk % 2 == 0:
+            continue
+        right = weights.at[0, pl.ds((chunk - 1) * WIDTH, 2 * WIDTH), :]
+
+        for a in range(4):
+            part = jnp.dot(carried[a], right[...], preferred_element_type=jnp.float32)
+            if chunk == 1:
+                total[a] = part
+            elif chunk < CHUNKS - 1:
+                total[a] = total[a] + part
+            else:
+                part = (total[a] + part) * normed[a].astype(jnp.float32)
+                normed[a] = part.astype(jnp.bfloat16)
+                stores.append(pltpu.make_async_copy(normed.at[a], out.at[a], out_sems.at[a]))
+                stores[-1].start()
     for chunk in range(CHUNKS):
         for hop in range(3):
             forward[chunk].wait_sent(hop, rows)
             back[chunk].wait_sent(hop, rows)
-    for hop in range(4):
+    for hop in range(5):
         gather.wait_sent(hop)
     for store in stores:
         store.wait()
@@ -392,13 +396,14 @@
             pltpu.VMEM((2, 2048, WIDTH), f32),
             pltpu.VMEM((4, 512, WIDTH), bf16),
             pltpu.VMEM((4, 512, WIDTH), f32),
-            pltpu.VMEM((CHUNKS, 2048, WIDTH), f32),
+            pltpu.VMEM((4, 512, 2 * WIDTH), bf16),
+            pltpu.VMEM((4, 512, 768), f32),
             *[pltpu.VMEM(s, bf16) for s in (sent, sent, half_way, landed)],
             *[pltpu.VMEM(s, bf16) for s in (sent, sent, half_way, landed)],
             pltpu.SemaphoreType.DMA((7,)),
-            pltpu.SemaphoreType.DMA((9,)),
+            pltpu.SemaphoreType.DMA((5,)),
             *[pltpu.SemaphoreType.DMA((6 * CHUNKS,)) for _ in range(2)],
-            *[pltpu.SemaphoreType.DMA((4,)) for _ in range(2)],
+            *[pltpu.SemaphoreType.DMA((5,)) for _ in range(2)],
         ],
         compiler_params=pltpu.CompilerParams(collective_id=0, has_side_effects=True, vmem_limit_bytes=56 << 20),
         name="monarch_mix",
@@ -422,7 +427,7 @@
             pl.BlockSpec((1, channels), lambda i: (0, 0)),
         ],
         out_specs=pl.BlockSpec((256, channels), lambda i: (i, 0)),
-        compiler_params=pltpu.CompilerParams(vmem_limit_bytes=32 << 20),
+        compiler_params=pltpu.CompilerParams(vmem_limit_bytes=60 << 20),
         name="project_out",
     )(hidden, weight, scale)
 

time: 110 us -> 102 us (0.927)
  Pallas kernels: 106 us -> 101 us
  local copies, waits for them, and re-layouts: 3.83 us -> 0 us
    pallas_call x1, Pallas kernels: 101 us -> 93.1 us  [mix(): pl.pallas_call(mix_kernel, out_shape=[jax.ShapeDtypeStruct((4, 512, 768),...]
    unnamed x6 -> x0, local copies, waits for them, and re-layouts: 3.83 us -> none
    pallas_call x1, Pallas kernels: 5.39 us -> 8.21 us  [project_out(): pl.pallas_call(project_kernel, grid=(n // 256,), out_shape=jax.ShapeDtype...]
where the time goes in v3:
time: 102 us; the launch traced here: 101 us
  Pallas kernels  101 us (99%)
    pallas_call x1, Pallas kernels, mix(): pl.pallas_call(mix_kernel, out_shape=[jax.ShapeDtypeStruct((4, 512, 768),...  93.1 us
    pallas_call x1, Pallas kernels, project_out(): pl.pallas_call(project_kernel, grid=(n // 256,), out_shape=jax.ShapeDtype...  8.21 us

profile of v3, /device:TPU:0, one launch (start us, length us, event | category | flops | bytes accessed | tf_op | source)
XLA Modules:
  0.0 101.4 jit_solution(4534393269882833087)
XLA Ops:
  0.0 93.1 %monarch_mix.1 = (bf16[4,512,768]{2,1,0:T(8,128)(2,1)}, bf16[768,768]{1,0:T(8,128)(2,1)}, f32[1,768]{1,0:T(1,128)}) custom-call(bf16[4,512,768]{2,1,0:T(8,128)(2,1)} %bitcast.4, f32[768]{0:T(1024)} %gain.1, bf16[4,512,512]{2,1,0:T(8,128)(2,1)} %block_w.1, bf16[4,512,512]{2,1,0:T(8,128)(2,1)} %stride_w.1, bf16[3,96,768]{2,1,0:T(8,128)(2,1)} %proj_w.1, ...), custom_call_target="tpu_custom_call" | custom-call | tf_op jit(solution)/shard_map/monarch_mix/pallas_call | solution.py:381
  93.2 8.2 %project_out.1 = bf16[2048,768]{1,0:T(8,128)(2,1)} custom-call(bf16[2048,768]{1,0:T(8,128)(2,1)} %bitcast.3, bf16[768,768]{1,0:T(8,128)(2,1)} %get-tuple-element.9.weight, f32[1,768]{1,0:T(1,128)} %get-tuple-element.10.scale), custom_call_target="tpu_custom_call" | custom-call | tf_op jit(solution)/shard_map/project_out/pallas_call | solution.py:420

commit v4 on v3

--- a/solution.py
+++ b/solution.py
@@ -381,9 +381,9 @@
     return pl.pallas_call(
         mix_kernel,
         out_shape=[
-            jax.ShapeDtypeStruct((4, 512, 768), bf16),
-            jax.ShapeDtypeStruct((768, 768), bf16),
-            jax.ShapeDtypeStruct((1, 768), f32),
+            pltpu.VMEM((4, 512, 768), bf16),
+            pltpu.VMEM((768, 768), bf16),
+            pltpu.VMEM((1, 768), f32),
         ],
         in_specs=[hbm, vmem, hbm, hbm, hbm, vmem],
         out_specs=[hbm, hbm, vmem],
@@ -405,31 +405,37 @@
             *[pltpu.SemaphoreType.DMA((6 * CHUNKS,)) for _ in range(2)],
             *[pltpu.SemaphoreType.DMA((5,)) for _ in range(2)],
         ],
-        compiler_params=pltpu.CompilerParams(collective_id=0, has_side_effects=True, vmem_limit_bytes=56 << 20),
+        compiler_params=pltpu.CompilerParams(collective_id=0, has_side_effects=True, vmem_limit_bytes=52 << 20),
         name="monarch_mix",
     )(tokens, gain, block_w, stride_w, proj_w, scales)
 
 
-def project_kernel(hidden, weight, scale, out):
-    product = jnp.dot(hidden[...], weight[...], preferred_element_type=jnp.float32)
-    out[...] = (product * scale[...]).astype(jnp.bfloat16)
+def project_kernel(hidden, weight, scale, out, result, sems):
+    stores = []
+    for i in range(4):
+        product = jnp.dot(hidden[i], weight[...], preferred_element_type=jnp.float32)
+        result[i] = (product * scale[...]).astype(jnp.bfloat16)
+        stores.append(pltpu.make_async_copy(result.at[i], out.at[i], sems.at[i]))
+        stores[-1].start()
+    for store in stores:
+        store.wait()
 
 
 def project_out(hidden, weight, scale):
-    n, channels = hidden.shape
+    vmem = pl.BlockSpec(memory_space=pltpu.VMEM)
     return pl.pallas_call(
         project_kernel,
-        grid=(n // 256,),
-        out_shape=jax.ShapeDtypeStruct((n, channels), jnp.bfloat16),
-        in_specs=[
-            pl.BlockSpec((256, channels), lambda i: (i, 0)),
-            pl.BlockSpec((channels, channels), lambda i: (0, 0)),
-            pl.BlockSpec((1, channels), lambda i: (0, 0)),
-        ],
-        out_specs=pl.BlockSpec((256, channels), lambda i: (i, 0)),
-        compiler_params=pltpu.CompilerParams(vmem_limit_bytes=60 << 20),
+        out_shape=jax.ShapeDtypeStruct(hidden.shape, jnp.bfloat16),
+        in_specs=[vmem, vmem, vmem],
+        out_specs=pl.BlockSpec(memory_space=pl.ANY),
+        scratch_shapes=[pltpu.VMEM(hidden.shape, jnp.bfloat16), pltpu.SemaphoreType.DMA((4,))],
+        compiler_params=pltpu.CompilerParams(vmem_limit_bytes=24 << 20),
         name="project_out",
-    )(hidden, weight, scale)
+    )(
+        pltpu.with_memory_space_constraint(hidden, pltpu.VMEM),
+        pltpu.with_memory_space_constraint(weight, pltpu.VMEM),
+        pltpu.with_memory_space_constraint(scale, pltpu.VMEM),
+    )
 
 
 def local(tokens, norm_gain, block_weights, stride_weights, proj_weights, proj_scales):
@@ -437,7 +443,7 @@
     hidden, out_weight, out_scale = mix(
         tokens.reshape(4, 512, channels), norm_gain, block_weights, stride_weights, proj_weights, proj_scales
     )
-    return project_out(hidden.reshape(2048, channels), out_weight, out_scale).reshape(tokens.shape)
+    return project_out(hidden, out_weight, out_scale).reshape(tokens.shape)
 
 
 def solution(mesh):

time: 102 us -> 96.5 us (0.946)
  Pallas kernels: 101 us -> 96.1 us
    pallas_call x2, Pallas kernels: 101 us -> 96.1 us  [the longest x1 92.6 us: mix(): pl.pallas_call(mix_kernel, out_shape=[pltpu.VMEM((4, 512, 768), bf16), pl...]
where the time goes in v4:
time: 96.5 us; the launch traced here: 96.3 us
  Pallas kernels  96.1 us (100%)
    pallas_call x1, Pallas kernels, mix(): pl.pallas_call(mix_kernel, out_shape=[pltpu.VMEM((4, 512, 768), bf16), pl...  92.6 us
    pallas_call x1, Pallas kernels, project_out(): pl.pallas_call(project_kernel, out_shape=jax.ShapeDtypeStruct(hidden.shap...  3.58 us

profile of v4, /device:TPU:0, one launch (start us, length us, event | category | flops | bytes accessed | tf_op | source)
XLA Modules:
  0.0 96.3 jit_solution(18061969577827693687)
XLA Ops:
  0.0 92.6 %monarch_mix.1 = (bf16[4,512,768]{2,1,0:T(8,128)(2,1)S(1)}, bf16[768,768]{1,0:T(8,128)(2,1)S(1)}, f32[1,768]{1,0:T(1,128)S(1)}) custom-call(bf16[4,512,768]{2,1,0:T(8,128)(2,1)} %bitcast.2, f32[768]{0:T(1024)} %gain.1, bf16[4,512,512]{2,1,0:T(8,128)(2,1)} %block_w.1, bf16[4,512,512]{2,1,0:T(8,128)(2,1)} %stride_w.1, bf16[3,96,768]{2,1,0:T(8,128)(2,1)} %proj_w.1, ...), custom_call_target="tpu_custom_call" | custom-call | tf_op jit(solution)/shard_map/monarch_mix/pallas_call | solution.py:381
  92.6 3.6 %project_out.1 = bf16[4,512,768]{2,1,0:T(8,128)(2,1)} custom-call(bf16[4,512,768]{2,1,0:T(8,128)(2,1)S(1)} %get-tuple-element.8.hidden, bf16[768,768]{1,0:T(8,128)(2,1)S(1)} %get-tuple-element.9.weight, f32[1,768]{1,0:T(1,128)S(1)} %get-tuple-element.10.scale), custom_call_target="tpu_custom_call" | custom-call | tf_op jit(solution)/shard_map/project_out/pallas_call | solution.py:426

commit v5 on v4

--- a/solution.py
+++ b/solution.py
@@ -215,6 +215,8 @@
     for offset in PARTNERS:
         pl.semaphore_signal(barrier, inc=1, device_id=neighbour(me, offset), device_id_type=MESH)
 
+    pl.semaphore_wait(barrier, len(PARTNERS))
+    gather.start(0)
     for b in range(4):
         loads[b].wait()
 
@@ -226,8 +228,6 @@
             return carry
 
         lax.fori_loop(0, 8, norm, 0)
-    pl.semaphore_wait(barrier, len(PARTNERS))
-    gather.start(0)
     loads[4].wait()
 
     forward = [Journey(me, c, (fwd0, fwd1, fwd2, fwd3), sems, 3 * c) for c in range(CHUNKS)]
@@ -238,13 +238,18 @@
     def paired(p, q):
         return jnp.where(low, p, pltpu.roll(q, 4, 0)), jnp.where(low, pltpu.roll(p, 4, 0), q)
 
-    for g in range(CHUNKS // 2):
+    for first, count in ((0, 2), (2, 1), (3, 1), (4, 2)):
+        if first == 3:
+            loads[6].wait()
+            gather.wait(0)
+            gather.start(1)
         for b in range(4):
-            x = jnp.dot(block_v[b], normed[b, :, pl.ds(g * 256, 256)], preferred_element_type=jnp.float32)
-            for half in range(2):
+            columns = pl.ds(first * WIDTH, count * WIDTH)
+            x = jnp.dot(block_v[b], normed[b, :, columns], preferred_element_type=jnp.float32)
+            for half in range(count):
                 wide[half, pl.ds(b, 512, stride=4), :] = x[:, half * WIDTH : (half + 1) * WIDTH]
-        for half in range(2):
-            chunk = 2 * g + half
+        for half in range(count):
+            chunk = first + half
 
             def pack(m, y_hi, z, core, half=half, chunk=chunk):
                 for x in range(4):
@@ -256,9 +261,6 @@
             each_octet(pack)
             forward[chunk].start(0)
 
-    loads[6].wait()
-    gather.wait(0)
-    gather.start(1)
     for hop in range(2):
         for chunk in range(CHUNKS):
             forward[chunk].wait(hop)

time: 96.5 us -> 101 us (1.047)
  Pallas kernels: 96.1 us -> 100 us
    pallas_call x1, Pallas kernels: 92.6 us -> 96.4 us  [mix(): pl.pallas_call(mix_kernel, out_shape=[pltpu.VMEM((4, 512, 768), bf16), pl...]
where the time goes in v5:
time: 101 us; the launch traced here: 100 us
  Pallas kernels  100 us (99%)
    pallas_call x1, Pallas kernels, mix(): pl.pallas_call(mix_kernel, out_shape=[pltpu.VMEM((4, 512, 768), bf16), pl...  96.4 us
    pallas_call x1, Pallas kernels, project_out(): pl.pallas_call(project_kernel, out_shape=jax.ShapeDtypeStruct(hidden.shap...  3.58 us

profile of v5, /device:TPU:0, one launch (start us, length us, event | category | flops | bytes accessed | tf_op | source)
XLA Modules:
  0.0 100.2 jit_solution(17541564277278775388)
XLA Ops:
  0.0 96.4 %monarch_mix.1 = (bf16[4,512,768]{2,1,0:T(8,128)(2,1)S(1)}, bf16[768,768]{1,0:T(8,128)(2,1)S(1)}, f32[1,768]{1,0:T(1,128)S(1)}) custom-call(bf16[4,512,768]{2,1,0:T(8,128)(2,1)} %bitcast.2, f32[768]{0:T(1024)} %gain.1, bf16[4,512,512]{2,1,0:T(8,128)(2,1)} %block_w.1, bf16[4,512,512]{2,1,0:T(8,128)(2,1)} %stride_w.1, bf16[3,96,768]{2,1,0:T(8,128)(2,1)} %proj_w.1, ...), custom_call_target="tpu_custom_call" | custom-call | tf_op jit(solution)/shard_map/monarch_mix/pallas_call | solution.py:383
  96.4 3.6 %project_out.1 = bf16[4,512,768]{2,1,0:T(8,128)(2,1)} custom-call(bf16[4,512,768]{2,1,0:T(8,128)(2,1)S(1)} %get-tuple-element.8.hidden, bf16[768,768]{1,0:T(8,128)(2,1)S(1)} %get-tuple-element.9.weight, f32[1,768]{1,0:T(1,128)S(1)} %get-tuple-element.10.scale), custom_call_target="tpu_custom_call" | custom-call | tf_op jit(solution)/shard_map/project_out/pallas_call | solution.py:428

commit v6 on v5

--- a/solution.py
+++ b/solution.py
@@ -12,6 +12,7 @@
 CHUNKS = len(ORDERS)
 WIDTH = 128
 PIECE = 16
+INNER, OUTER = pl.ds(0, 2), pl.ds(2, 1)
 
 
 def coordinates():
@@ -107,34 +108,50 @@
     def shard(self, h, first=0, rows=96):
         return self.weights.at[:, pl.ds(pl.multiple_of(h * 96 + first, PIECE), rows), :]
 
-    def part(self, h, first=0, rows=96):
-        return self.weights.at[:, pl.ds(pl.multiple_of(h * 96 + first, PIECE), rows), self.columns]
+    def part(self, h, first, rows, which):
+        return self.weights.at[which, pl.ds(pl.multiple_of(h * 96 + first, PIECE), rows), self.columns]
 
     def copies(self, hop):
         me, x = self.me, self.x
         half = (me[2] % 2) * 48
         if hop == 0:
             for first, step in ((0, 1), (48, 3)):
-                yield self.proj_w.at[:, pl.ds(first, 48), self.columns], self.part(self.mine, first, 48), along(1, step)
+                yield self.proj_w.at[INNER, pl.ds(first, 48), self.columns], self.part(self.mine, first, 48, INNER), along(1, step)
         elif hop == 1:
             for step in (1, 3):
                 for y_lo in range(2):
-                    ref = self.part(x * 2 + y_lo, half, 48)
+                    ref = self.part(x * 2 + y_lo, half, 48, INNER)
                     yield ref, ref, along(0, step)
+                ref = self.part(self.mine, half, 48, OUTER)
+                yield ref, ref, along(0, step)
         elif hop == 2:
             for y_lo, step in ((0, 1), (1, 3)):
-                ref = self.part(((x + 4 - step) % 4) * 2 + y_lo, half, 48)
+                ref = self.part(((x + 4 - step) % 4) * 2 + y_lo, half, 48, INNER)
                 yield ref, ref, along(0, step)
+            step = 1 + 2 * me[3]
+            ref = self.part(((x + 4 - step) % 4) * 2 + self.y_lo, half, 48, OUTER)
+            yield ref, ref, along(0, step)
         elif hop == 3:
             for other in (1, 2, 3):
                 for y_lo, step in ((0, 1), (1, 3)):
-                    ref = self.part(((x + other) % 4) * 2 + y_lo, half, 48)
+                    ref = self.part(((x + other) % 4) * 2 + y_lo, half, 48, INNER)
                     yield ref, ref, along(2, step)
-        else:
-            ref = self.part(x * 2 + 1 - self.y_lo)
+                ref = self.part(((x + other) % 4) * 2 + self.y_lo, half, 48, OUTER)
+                yield ref, ref, along(2, 1 + 2 * ((other + me[3]) % 2))
+        elif hop == 4:
+            for other, step in enumerate((1, 3, 1, 3)):
+                ref = self.part(other * 2 + self.y_lo, 0, 96, OUTER)
+                yield ref, ref, along(1, step)
+            ref = self.part(x * 2 + 1 - self.y_lo, 0, 96, INNER)
             yield ref, ref, (0, 0, 0, 1)
             for other in (1, 2, 3):
-                ref = self.part(((x + other) % 4) * 2, 0, 192)
+                ref = self.part(((x + other) % 4) * 2, 0, 192, INNER)
+                yield ref, ref, (0, 0, 0, 1)
+        else:
+            ref = self.part(x * 2 + 1 - self.y_lo, 0, 96, OUTER)
+            yield ref, ref, (0, 0, 0, 1)
+            for other in (1, 2, 3):
+                ref = self.part(((x + other) % 4) * 2, 0, 192, OUTER)
                 yield ref, ref, (0, 0, 0, 1)
 
     def start(self, hop):
@@ -149,7 +166,7 @@
             ).start()
 
     def _wait(self, sems, hop):
-        ref = self.weights.at[:, pl.ds(0, (96, 192, 96, 288, 672)[hop]), pl.ds(0, 384)]
+        ref = self.weights.at[:, pl.ds(0, (64, 160, 80, 240, 576, 224)[hop]), pl.ds(0, 384)]
         pltpu.make_async_copy(ref, ref, sems.at[hop]).wait()
 
     def wait(self, hop):
@@ -174,10 +191,9 @@
     stride_w,
     proj_w,
     scales,
-    out,
+    normed,
     out_proj,
     out_scale,
-    normed,
     block_v,
     stride_v,
     weights,
@@ -196,7 +212,7 @@
     ret2,
     ret3,
     load_sems,
-    out_sems,
+    out_sem,
     send_sems,
     recv_sems,
     gather_send,
@@ -209,14 +225,12 @@
     loads.append(pltpu.make_async_copy(stride_w, stride_v, load_sems.at[5]))
     gather = Gather(me, proj_w, weights, gather_send, gather_recv)
     loads.append(pltpu.make_async_copy(proj_w, gather.shard(gather.mine), load_sems.at[6]))
-    for load in loads:
+    for load in loads[:5]:
         load.start()
     barrier = pltpu.get_barrier_semaphore()
     for offset in PARTNERS:
         pl.semaphore_signal(barrier, inc=1, device_id=neighbour(me, offset), device_id_type=MESH)
 
-    pl.semaphore_wait(barrier, len(PARTNERS))
-    gather.start(0)
     for b in range(4):
         loads[b].wait()
 
@@ -228,7 +242,11 @@
             return carry
 
         lax.fori_loop(0, 8, norm, 0)
+    pl.semaphore_wait(barrier, len(PARTNERS))
+    gather.start(0)
     loads[4].wait()
+    for load in loads[5:]:
+        load.start()
 
     forward = [Journey(me, c, (fwd0, fwd1, fwd2, fwd3), sems, 3 * c) for c in range(CHUNKS)]
     back = [Journey(me, c, (ret0, ret1, ret2, ret3), sems, 3 * (CHUNKS + c)) for c in range(CHUNKS)]
@@ -239,10 +257,6 @@
         return jnp.where(low, p, pltpu.roll(q, 4, 0)), jnp.where(low, pltpu.roll(p, 4, 0), q)
 
     for first, count in ((0, 2), (2, 1), (3, 1), (4, 2)):
-        if first == 3:
-            loads[6].wait()
-            gather.wait(0)
-            gather.start(1)
         for b in range(4):
             columns = pl.ds(first * WIDTH, count * WIDTH)
             x = jnp.dot(block_v[b], normed[b, :, columns], preferred_element_type=jnp.float32)
@@ -261,6 +275,9 @@
             each_octet(pack)
             forward[chunk].start(0)
 
+    loads[6].wait()
+    gather.wait(0)
+    gather.start(1)
     for hop in range(2):
         for chunk in range(CHUNKS):
             forward[chunk].wait(hop)
@@ -309,18 +326,19 @@
         back[chunk].wait(0)
         back[chunk].start(1)
     gather.wait(4)
-    for k in range(3):
-
-        def add_squares(i, sums, k=k):
+    gather.start(5)
+
+    def scale_columns(k):
+        def add_squares(i, sums):
             w = weights[k, pl.ds(pl.multiple_of(i * 64, 64), 64), :].astype(jnp.float32)
             return sums + jnp.sum((w * w).reshape(8, 8, 768), axis=0)
 
         sums = lax.fori_loop(0, 12, add_squares, jnp.zeros((8, 768), jnp.float32))
         squares = jnp.sum(sums, axis=0, keepdims=True)
         colscale[pl.ds(k, 1), :] = scales[pl.ds(k, 1), :] * lax.rsqrt(squares + 1e-06)
-    out_scale[...] = colscale[pl.ds(2, 1), :]
-    stores = [pltpu.make_async_copy(weights.at[2], out_proj, out_sems.at[4])]
-    stores[0].start()
+
+    scale_columns(0)
+    scale_columns(1)
 
     def gate_block(i):
         r = pl.ds((i % 2) * 256, 256)
@@ -329,11 +347,16 @@
         gate = gate / (1.0 + jnp.exp(-gate)) * colscale[pl.ds(0, 1), :]
         normed[i // 2, r, :] = gate.astype(jnp.bfloat16)
 
+    for i in range(8):
+        gate_block(i)
     for chunk in range(CHUNKS):
         back[chunk].wait(1)
         back[chunk].start(2)
-        for i in ((0, 1), (2, 3), (4,), (5,), (6,), (7,))[chunk]:
-            gate_block(i)
+    gather.wait(5)
+    scale_columns(2)
+    out_scale[...] = colscale[pl.ds(2, 1), :]
+    store = pltpu.make_async_copy(weights.at[2], out_proj, out_sem)
+    store.start()
 
     for chunk in range(CHUNKS):
         back[chunk].wait(2)
@@ -362,16 +385,13 @@
             else:
                 part = (total[a] + part) * normed[a].astype(jnp.float32)
                 normed[a] = part.astype(jnp.bfloat16)
-                stores.append(pltpu.make_async_copy(normed.at[a], out.at[a], out_sems.at[a]))
-                stores[-1].start()
     for chunk in range(CHUNKS):
         for hop in range(3):
             forward[chunk].wait_sent(hop, rows)
             back[chunk].wait_sent(hop, rows)
-    for hop in range(5):
+    for hop in range(6):
         gather.wait_sent(hop)
-    for store in stores:
-        store.wait()
+    store.wait()
 
 
 def mix(tokens, gain, block_w, stride_w, proj_w, scales):
@@ -388,9 +408,8 @@
             pltpu.VMEM((1, 768), f32),
         ],
         in_specs=[hbm, vmem, hbm, hbm, hbm, vmem],
-        out_specs=[hbm, hbm, vmem],
+        out_specs=[vmem, hbm, vmem],
         scratch_shapes=[
-            pltpu.VMEM((4, 512, 768), bf16),
             pltpu.VMEM((4, 512, 512), bf16),
             pltpu.VMEM((4, 512, 512), bf16),
             pltpu.VMEM((3, 768, 768), bf16),
@@ -403,9 +422,9 @@
             *[pltpu.VMEM(s, bf16) for s in (sent, sent, half_way, landed)],
             *[pltpu.VMEM(s, bf16) for s in (sent, sent, half_way, landed)],
             pltpu.SemaphoreType.DMA((7,)),
-            pltpu.SemaphoreType.DMA((5,)),
+            pltpu.SemaphoreType.DMA,
             *[pltpu.SemaphoreType.DMA((6 * CHUNKS,)) for _ in range(2)],
-            *[pltpu.SemaphoreType.DMA((5,)) for _ in range(2)],
+            *[pltpu.SemaphoreType.DMA((6,)) for _ in range(2)],
         ],
         compiler_params=pltpu.CompilerParams(collective_id=0, has_side_effects=True, vmem_limit_bytes=52 << 20),
         name="monarch_mix",

time: 101 us -> 94.3 us (0.934)
  Pallas kernels: 100 us -> 94 us
    pallas_call x1, Pallas kernels: 96.4 us -> 90.4 us  [mix(): pl.pallas_call(mix_kernel, out_shape=[pltpu.VMEM((4, 512, 768), bf16), pl...]
where the time goes in v6:
time: 94.3 us; the launch traced here: 94.1 us
  Pallas kernels  94 us (100%)
    pallas_call x1, Pallas kernels, mix(): pl.pallas_call(mix_kernel, out_shape=[pltpu.VMEM((4, 512, 768), bf16), pl...  90.4 us
    pallas_call x1, Pallas kernels, project_out(): pl.pallas_call(project_kernel, out_shape=jax.ShapeDtypeStruct(hidden.shap...  3.59 us

profile of v6, /device:TPU:0, one launch (start us, length us, event | category | flops | bytes accessed | tf_op | source)
XLA Modules:
  0.0 94.1 jit_solution(15322945992901216524)
XLA Ops:
  0.0 90.4 %monarch_mix.1 = (bf16[4,512,768]{2,1,0:T(8,128)(2,1)S(1)}, bf16[768,768]{1,0:T(8,128)(2,1)S(1)}, f32[1,768]{1,0:T(1,128)S(1)}) custom-call(bf16[4,512,768]{2,1,0:T(8,128)(2,1)} %bitcast.2, f32[768]{0:T(1024)} %gain.1, bf16[4,512,512]{2,1,0:T(8,128)(2,1)} %block_w.1, bf16[4,512,512]{2,1,0:T(8,128)(2,1)} %stride_w.1, bf16[3,96,768]{2,1,0:T(8,128)(2,1)} %proj_w.1, ...), custom_call_target="tpu_custom_call" | custom-call | tf_op jit(solution)/shard_map/monarch_mix/pallas_call | solution.py:403
  90.4 3.6 %project_out.1 = bf16[4,512,768]{2,1,0:T(8,128)(2,1)} custom-call(bf16[4,512,768]{2,1,0:T(8,128)(2,1)S(1)} %get-tuple-element.8.hidden, bf16[768,768]{1,0:T(8,128)(2,1)S(1)} %get-tuple-element.9.weight, f32[1,768]{1,0:T(1,128)S(1)} %get-tuple-element.10.scale), custom_call_target="tpu_custom_call" | custom-call | tf_op jit(solution)/shard_map/project_out/pallas_call | solution.py:447

commit v7 on v6

--- a/solution.py
+++ b/solution.py
@@ -12,6 +12,7 @@
 CHUNKS = len(ORDERS)
 WIDTH = 128
 PIECE = 16
+GROUPS = ((0, 1, 2), (3, 4, 5))
 INNER, OUTER = pl.ds(0, 2), pl.ds(2, 1)
 
 
@@ -117,12 +118,12 @@
         if hop == 0:
             for first, step in ((0, 1), (48, 3)):
                 yield self.proj_w.at[INNER, pl.ds(first, 48), self.columns], self.part(self.mine, first, 48, INNER), along(1, step)
+            mine = pl.ds(pl.multiple_of(half, PIECE), 48)
+            for step in (1, 3):
+                yield self.proj_w.at[:, mine, self.columns], self.part(self.mine, half, 48, slice(None)), along(0, step)
         elif hop == 1:
             for step in (1, 3):
-                for y_lo in range(2):
-                    ref = self.part(x * 2 + y_lo, half, 48, INNER)
-                    yield ref, ref, along(0, step)
-                ref = self.part(self.mine, half, 48, OUTER)
+                ref = self.part(x * 2 + 1 - self.y_lo, half, 48, INNER)
                 yield ref, ref, along(0, step)
         elif hop == 2:
             for y_lo, step in ((0, 1), (1, 3)):
@@ -166,7 +167,7 @@
             ).start()
 
     def _wait(self, sems, hop):
-        ref = self.weights.at[:, pl.ds(0, (64, 160, 80, 240, 576, 224)[hop]), pl.ds(0, 384)]
+        ref = self.weights.at[:, pl.ds(0, (160, 64, 80, 240, 576, 224)[hop]), pl.ds(0, 384)]
         pltpu.make_async_copy(ref, ref, sems.at[hop]).wait()
 
     def wait(self, hop):
@@ -225,23 +226,31 @@
     loads.append(pltpu.make_async_copy(stride_w, stride_v, load_sems.at[5]))
     gather = Gather(me, proj_w, weights, gather_send, gather_recv)
     loads.append(pltpu.make_async_copy(proj_w, gather.shard(gather.mine), load_sems.at[6]))
-    for load in loads[:5]:
+    for load in loads[:4]:
         load.start()
     barrier = pltpu.get_barrier_semaphore()
     for offset in PARTNERS:
         pl.semaphore_signal(barrier, inc=1, device_id=neighbour(me, offset), device_id_type=MESH)
 
+    loads[4].start()
+
     for b in range(4):
         loads[b].wait()
 
         def norm(i, carry, b=b):
-            r = pl.ds(pl.multiple_of(i * 64, 64), 64)
-            x = normed[b, r, :].astype(jnp.float32)
-            scale = lax.rsqrt(jnp.mean(x * x, axis=-1, keepdims=True) + 1e-05)
-            normed[b, r, :] = (x * scale * gain[...][None, :]).astype(jnp.bfloat16)
+            r = pl.ds(pl.multiple_of(i * 128, 128), 128)
+            tiles = [pl.ds(n * WIDTH, WIDTH) for n in range(CHUNKS)]
+            squares = jnp.zeros((128, WIDTH), jnp.float32)
+            for c in tiles:
+                x = normed[b, r, c].astype(jnp.float32)
+                squares = squares + x * x
+            scale = lax.rsqrt(jnp.sum(squares, axis=-1, keepdims=True) / 768 + 1e-05)
+            for c in tiles:
+                x = normed[b, r, c].astype(jnp.float32)
+                normed[b, r, c] = (x * scale * gain[c][None, :]).astype(jnp.bfloat16)
             return carry
 
-        lax.fori_loop(0, 8, norm, 0)
+        lax.fori_loop(0, 4, norm, 0)
     pl.semaphore_wait(barrier, len(PARTNERS))
     gather.start(0)
     loads[4].wait()
@@ -256,7 +265,7 @@
     def paired(p, q):
         return jnp.where(low, p, pltpu.roll(q, 4, 0)), jnp.where(low, pltpu.roll(p, 4, 0), q)
 
-    for first, count in ((0, 2), (2, 1), (3, 1), (4, 2)):
+    for first, count in ((0, 2), (2, 2), (4, 2)):
         for b in range(4):
             columns = pl.ds(first * WIDTH, count * WIDTH)
             x = jnp.dot(block_v[b], normed[b, :, columns], preferred_element_type=jnp.float32)
@@ -369,22 +378,21 @@
                     wide[chunk % 2, r, :] = ret3[(chunk, *slot)].astype(jnp.float32)
 
         each_octet(unpack)
+        group = [g for g in GROUPS if chunk in g][0]
+        place = pl.ds((chunk - group[0]) * WIDTH, WIDTH)
         for a in range(4):
-            part = wide[chunk % 2, pl.ds(a, 512, stride=4), :].astype(jnp.bfloat16)
-            carried[a, :, pl.ds(chunk % 2 * WIDTH, WIDTH)] = part
-        if chunk % 2 == 0:
+            carried[a, :, place] = wide[chunk % 2, pl.ds(a, 512, stride=4), :].astype(jnp.bfloat16)
+        if chunk != group[-1]:
             continue
-        right = weights.at[0, pl.ds((chunk - 1) * WIDTH, 2 * WIDTH), :]
-
+        left, right = pl.ds(0, len(group) * WIDTH), pl.ds(group[0] * WIDTH, len(group) * WIDTH)
         for a in range(4):
-            part = jnp.dot(carried[a], right[...], preferred_element_type=jnp.float32)
-            if chunk == 1:
+            part = jnp.dot(carried[a, :, left], weights[0, right, :], preferred_element_type=jnp.float32)
+            if group != GROUPS[0]:
+                part = total[a] + part
+            if group == GROUPS[-1]:
+                normed[a] = (part * normed[a].astype(jnp.float32)).astype(jnp.bfloat16)
+            else:
                 total[a] = part
-            elif chunk < CHUNKS - 1:
-                total[a] = total[a] + part
-            else:
-                part = (total[a] + part) * normed[a].astype(jnp.float32)
-                normed[a] = part.astype(jnp.bfloat16)
     for chunk in range(CHUNKS):
         for hop in range(3):
             forward[chunk].wait_sent(hop, rows)
@@ -417,7 +425,7 @@
             pltpu.VMEM((2, 2048, WIDTH), f32),
             pltpu.VMEM((4, 512, WIDTH), bf16),
             pltpu.VMEM((4, 512, WIDTH), f32),
-            pltpu.VMEM((4, 512, 2 * WIDTH), bf16),
+            pltpu.VMEM((4, 512, 3 * WIDTH), bf16),
             pltpu.VMEM((4, 512, 768), f32),
             *[pltpu.VMEM(s, bf16) for s in (sent, sent, half_way, landed)],
             *[pltpu.VMEM(s, bf16) for s in (sent, sent, half_way, landed)],

time: 94.3 us -> 93.3 us (0.989)
  Pallas kernels: 94 us -> 92.6 us
    pallas_call x1, Pallas kernels: 90.4 us -> 89.1 us  [mix(): pl.pallas_call(mix_kernel, out_shape=[pltpu.VMEM((4, 512, 768), bf16), pl...]
where the time goes in v7:
time: 93.3 us; the launch traced here: 92.8 us
  Pallas kernels  92.6 us (99%)
    pallas_call x1, Pallas kernels, mix(): pl.pallas_call(mix_kernel, out_shape=[pltpu.VMEM((4, 512, 768), bf16), pl...  89.1 us
    pallas_call x1, Pallas kernels, project_out(): pl.pallas_call(project_kernel, out_shape=jax.ShapeDtypeStruct(hidden.shap...  3.59 us

profile of v7, /device:TPU:0, one launch (start us, length us, event | category | flops | bytes accessed | tf_op | source)
XLA Modules:
  0.0 92.8 jit_solution(7747396236945158303)
XLA Ops:
  0.0 89.1 %monarch_mix.1 = (bf16[4,512,768]{2,1,0:T(8,128)(2,1)S(1)}, bf16[768,768]{1,0:T(8,128)(2,1)S(1)}, f32[1,768]{1,0:T(1,128)S(1)}) custom-call(bf16[4,512,768]{2,1,0:T(8,128)(2,1)} %bitcast.2, f32[768]{0:T(1024)} %gain.1, bf16[4,512,512]{2,1,0:T(8,128)(2,1)} %block_w.1, bf16[4,512,512]{2,1,0:T(8,128)(2,1)} %stride_w.1, bf16[3,96,768]{2,1,0:T(8,128)(2,1)} %proj_w.1, ...), custom_call_target="tpu_custom_call" | custom-call | tf_op jit(solution)/shard_map/monarch_mix/pallas_call | solution.py:411
  89.1 3.6 %project_out.1 = bf16[4,512,768]{2,1,0:T(8,128)(2,1)} custom-call(bf16[4,512,768]{2,1,0:T(8,128)(2,1)S(1)} %get-tuple-element.8.hidden, bf16[768,768]{1,0:T(8,128)(2,1)S(1)} %get-tuple-element.9.weight, f32[1,768]{1,0:T(1,128)S(1)} %get-tuple-element.10.scale), custom_call_target="tpu_custom_call" | custom-call | tf_op jit(solution)/shard_map/project_out/pallas_call | solution.py:455

commit v8 on v7

--- a/solution.py
+++ b/solution.py
@@ -441,10 +441,11 @@
 
 def project_kernel(hidden, weight, scale, out, result, sems):
     stores = []
-    for i in range(4):
-        product = jnp.dot(hidden[i], weight[...], preferred_element_type=jnp.float32)
-        result[i] = (product * scale[...]).astype(jnp.bfloat16)
-        stores.append(pltpu.make_async_copy(result.at[i], out.at[i], sems.at[i]))
+    for i in range(8):
+        r = pl.ds(i % 2 * 256, 256)
+        product = jnp.dot(hidden[i // 2, r, :], weight[...], preferred_element_type=jnp.float32)
+        result[i // 2, r, :] = (product * scale[...]).astype(jnp.bfloat16)
+        stores.append(pltpu.make_async_copy(result.at[i // 2, r], out.at[i // 2, r], sems.at[i]))
         stores[-1].start()
     for store in stores:
         store.wait()
@@ -457,7 +458,7 @@
         out_shape=jax.ShapeDtypeStruct(hidden.shape, jnp.bfloat16),
         in_specs=[vmem, vmem, vmem],
         out_specs=pl.BlockSpec(memory_space=pl.ANY),
-        scratch_shapes=[pltpu.VMEM(hidden.shape, jnp.bfloat16), pltpu.SemaphoreType.DMA((4,))],
+        scratch_shapes=[pltpu.VMEM(hidden.shape, jnp.bfloat16), pltpu.SemaphoreType.DMA((8,))],
         compiler_params=pltpu.CompilerParams(vmem_limit_bytes=24 << 20),
         name="project_out",
     )(

time: 93.3 us -> 93.1 us (level)
  no operation moved by 1% of the time
where the time goes in v8:
time: 93.1 us; the launch traced here: 92.7 us
  Pallas kernels  92.5 us (99%)
    pallas_call x1, Pallas kernels, mix(): pl.pallas_call(mix_kernel, out_shape=[pltpu.VMEM((4, 512, 768), bf16), pl...  89.1 us
    pallas_call x1, Pallas kernels, project_out(): pl.pallas_call(project_kernel, out_shape=jax.ShapeDtypeStruct(hidden.shap...  3.44 us

profile of v8, /device:TPU:0, one launch (start us, length us, event | category | flops | bytes accessed | tf_op | source)
XLA Modules:
  0.0 92.7 jit_solution(11340727860467954919)
XLA Ops:
  0.0 89.1 %monarch_mix.1 = (bf16[4,512,768]{2,1,0:T(8,128)(2,1)S(1)}, bf16[768,768]{1,0:T(8,128)(2,1)S(1)}, f32[1,768]{1,0:T(1,128)S(1)}) custom-call(bf16[4,512,768]{2,1,0:T(8,128)(2,1)} %bitcast.2, f32[768]{0:T(1024)} %gain.1, bf16[4,512,512]{2,1,0:T(8,128)(2,1)} %block_w.1, bf16[4,512,512]{2,1,0:T(8,128)(2,1)} %stride_w.1, bf16[3,96,768]{2,1,0:T(8,128)(2,1)} %proj_w.1, ...), custom_call_target="tpu_custom_call" | custom-call | tf_op jit(solution)/shard_map/monarch_mix/pallas_call | solution.py:411
  89.1 3.4 %project_out.1 = bf16[4,512,768]{2,1,0:T(8,128)(2,1)} custom-call(bf16[4,512,768]{2,1,0:T(8,128)(2,1)S(1)} %get-tuple-element.8.hidden, bf16[768,768]{1,0:T(8,128)(2,1)S(1)} %get-tuple-element.9.weight, f32[1,768]{1,0:T(1,128)S(1)} %get-tuple-element.10.scale), custom_call_target="tpu_custom_call" | custom-call | tf_op jit(solution)/shard_map/project_out/pallas_call | solution.py:456
